TPU v7x, 32 devices: a whole 2x2x4 slice. The times are simulated.
32 devices in a mesh: dp: 8 (over z, y), shard: 4 (over x, core).
Axes of the slice: x: 2, y: 2, z: 4, core: 2. Of those that a mesh axis runs over, the one named last changes fastest.
Arguments:
- tokens: bfloat16 [16, 4096, 512], P('dp', 'shard'), may hold values from -6 to 6
- cotangent: bfloat16 [16, 4096, 512], P('dp', 'shard'), may hold values from -6 to 6
- segments: int32 [16, 4096], P('dp', 'shard'), may hold values from 0 to 4, as said below
- log_decay: float32 [2], replicated, may hold values from -0.034 to 0, as said below
- w_qk: float32 [2, 512, 512], P(None, 'shard'), may hold values from -0.25 to 0.25
- w_vg: float32 [2, 512, 864], P(None, 'shard'), may hold values from -0.25 to 0.25
- w_out: float32 [864, 512], P(None, 'shard'), may hold values from -0.21875 to 0.21875
- w_gu: float32 [2, 512, 864], P(None, 'shard'), may hold values from -0.25 to 0.25
- w_down: float32 [864, 512], P(None, 'shard'), may hold values from -0.21875 to 0.21875
- norm_gains: float32 [2, 512], P(None, 'shard'), may hold values from 0.5 to 1.4
- m_qk: float32 [2, 512, 512], P(None, 'shard'), may hold values from -0.0007324219 to 0.0007324219
- m_vg: float32 [2, 512, 864], P(None, 'shard'), may hold values from -0.0007324219 to 0.0007324219
- m_out: float32 [864, 512], P(None, 'shard'), may hold values from -0.0009765625 to 0.0009765625
- m_gu: float32 [2, 512, 864], P(None, 'shard'), may hold values from -0.0009765625 to 0.0009765625
- m_down: float32 [864, 512], P(None, 'shard'), may hold values from -0.0012207031 to 0.0012207031
- m_gains: float32 [2, 512], P(None, 'shard'), may hold values from -0.0014648438 to 0.0014648438
- v_qk: float32 [2, 512, 512], P(None, 'shard'), may hold values from 1.0693438e-08 to 4.2459238e-08
- v_vg: float32 [2, 512, 864], P(None, 'shard'), may hold values from 1.0693438e-08 to 4.2459238e-08
- v_out: float32 [864, 512], P(None, 'shard'), may hold values from 2.390298e-08 to 9.4353865e-08
- v_gu: float32 [2, 512, 864], P(None, 'shard'), may hold values from 1.6669183e-08 to 6.6047704e-08
- v_down: float32 [864, 512], P(None, 'shard'), may hold values from 2.7991646e-08 to 1.1322464e-07
- v_gains: float32 [2, 512], P(None, 'shard'), may hold values from 4.2459238e-08 to 1.6983695e-07
Outputs:
- tokens_out: bfloat16 [16, 4096, 512], P('dp', 'shard')
- grad_input: bfloat16 [16, 4096, 512], P('dp', 'shard')
- new_w_qk: float32 [2, 512, 512], P(None, 'shard')
- new_w_vg: float32 [2, 512, 864], P(None, 'shard')
- new_w_out: float32 [864, 512], P(None, 'shard')
- new_w_gu: float32 [2, 512, 864], P(None, 'shard')
- new_w_down: float32 [864, 512], P(None, 'shard')
- new_gains: float32 [2, 512], P(None, 'shard')
- new_m_qk: float32 [2, 512, 512], P(None, 'shard')
- new_m_vg: float32 [2, 512, 864], P(None, 'shard')
- new_m_out: float32 [864, 512], P(None, 'shard')
- new_m_gu: float32 [2, 512, 864], P(None, 'shard')
- new_m_down: float32 [864, 512], P(None, 'shard')
- new_m_gains: float32 [2, 512], P(None, 'shard')
- new_v_qk: float32 [2, 512, 512], P(None, 'shard')
- new_v_vg: float32 [2, 512, 864], P(None, 'shard')
- new_v_out: float32 [864, 512], P(None, 'shard')
- new_v_gu: float32 [2, 512, 864], P(None, 'shard')
- new_v_down: float32 [864, 512], P(None, 'shard')
- new_v_gains: float32 [2, 512], P(None, 'shard')
- grad_norm: float32 [], replicated
Inputs may be any that keep to these rules, and one draw needn't show every extreme that they name: `segments`: document numbers never fall along a sequence; each sequence holds exactly five documents, one of which begins before position 1024 and ends after position 3072. `log_decay`: negative.
All inputs are finite; a program needn't handle non-finite values.
Results may differ from a plain program's by a relative error of at most 0.02.
The roundings to bfloat16 on the way count: a program that leaves them out, or rounds other values in their place, can miss the bound.
Values may be sent and summed in bfloat16 or wider, within the bound.
No kernel may reach another device: no remote copies, remote signals or barrier semaphores. Data moves between devices by JAX's collectives and lax.ppermute only.
A program may use at most 256 MiB of HBM per device.

v0:
```python
import functools
import math

import jax
import jax.numpy as jnp
from jax import lax
from jax.experimental import pallas as pl
from jax.experimental.pallas import tpu as pltpu
from jax.sharding import PartitionSpec as P

H = 2
KD = 256
VD = 432
VP = 512
BLOCK = 512
STEP = 10

EPS = 1e-05
ADAM_EPS = 1e-08
BETA_ONE = 0.9
BETA_TWO = 0.95
MATRIX_RATE = 0.15
GAIN_RATE = 1.0
DECAY_WEIGHT = 0.1
CLIP = 1.0

LOW = jnp.bfloat16
WIDE = jnp.float32
VMEM = pltpu.VMEM
SMEM = pltpu.SMEM
MIB = 1024 * 1024


def dot(a, b):
    return jnp.dot(a, b, preferred_element_type=WIDE)


def dot_nt(a, b):
    return lax.dot_general(a, b, (((1,), (1,)), ((), ())), preferred_element_type=WIDE)


def dot_tn(a, b):
    return lax.dot_general(a, b, (((0,), (0,)), ((), ())), preferred_element_type=WIDE)


def params(size):
    return pltpu.CompilerParams(vmem_limit_bytes=size * MIB)


def cost(flops, moved):
    return pl.CostEstimate(flops=int(flops), bytes_accessed=int(moved), transcendentals=0)


def smem():
    return pl.BlockSpec(memory_space=SMEM)


def whole(shape):
    return pl.BlockSpec(shape, lambda *at: (0,) * len(shape), pipeline_mode=pl.Buffered(1))


def shape(dims, kind):
    return jax.ShapeDtypeStruct(dims, kind)


def bits_of(axis):
    return (lax.axis_size(axis) - 1).bit_length()


def exchange(value, axis, bit):
    size = lax.axis_size(axis)
    return lax.ppermute(value, axis, [(i, i ^ (1 << bit)) for i in range(size)])


def gather_shards(own):
    held = [(0, own)]
    for bit in reversed(range(bits_of("shard"))):
        held += [(mask | (1 << bit), exchange(part, "shard", bit)) for mask, part in held]
    return [(mask, None, part) for mask, part in held]


def add_low(one, two):
    return (one.astype(WIDE) + two.astype(WIDE)).astype(LOW)


class Reduction:
    def __init__(self, keep, send, halved):
        self.keep = keep
        self.near = exchange(send, "shard", 0)
        self.halved = halved
        self.stage = 0

    def cross(self, *done):
        self.near = after(self.near, *done)
        low = add_low(self.keep[1], self.near[1])
        self.got = exchange(low, "shard", 1)
        self.terms = [self.keep[0], self.near[0]]
        return low

    def next(self, *done):
        got = after(self.got, *done)
        count = bits_of("dp")
        rows = got.shape[0]

        def total(at):
            return sum(term[at].astype(WIDE) for term in (*self.terms, got)).astype(LOW)

        bit = self.stage
        if self.stage < count:
            if bit in self.halved:
                sent = total(slice(rows // 2, rows))
                self.terms = [total(slice(0, rows // 2))]
            else:
                sent = total(slice(0, rows))
                self.terms = [sent]
        else:
            bit = self.halved[count - 1 - self.stage]
            if self.stage == count:
                sent = total(slice(0, rows))
            else:
                sent = jnp.concatenate([self.held, got])
            self.held = sent
        self.stage += 1
        self.got = exchange(sent, "dp", bit)
        return sent

    def left(self):
        return bits_of("dp") + len(self.halved) - self.stage

    def result(self):
        return self.held, self.got


class Passing:
    def __init__(self, local, reverse):
        self.local = local
        steps = [[(0, 1), (2, 3)], [(1, 2)], [(2, 3)]]
        if reverse:
            steps = [[(3 - a, 3 - b) for a, b in step] for step in steps]
        self.steps = steps
        self.got = [lax.ppermute(local, "shard", steps[0])]

    def turn(self, decay, length, *done):
        self.got[0] = after(self.got[0], *done)
        total = combine(decay, length, self.local, self.got[0])
        self.got.append(lax.ppermute(total, "shard", self.steps[1]))
        return total

    def finish(self, *done):
        self.got.append(lax.ppermute(after(self.got[1], *done), "shard", self.steps[2]))


def entering(decay, length, h, got):
    factor = jnp.exp(jnp.full((1, 1), decay[h] * length, WIDE))
    wide = [item[h].astype(WIDE) for item in got]
    return wide[0] + wide[1] + factor * wide[2]


def after(value, *others):
    return lax.optimization_barrier((value, *others))[0]


def combine_kernel(length, decay, local, got, out):
    h = pl.program_id(0) % H
    factor = jnp.exp(jnp.full((1, 1), decay[h] * length, WIDE))
    out[...] = (local[...].astype(WIDE) + factor * got[...].astype(WIDE)).astype(LOW)


def combine(decay, length, local, got):
    block = pl.BlockSpec((None, None, KD, VP), lambda i: (i // H, i % H, 0, 0))
    return pl.pallas_call(
        functools.partial(combine_kernel, length),
        grid=(local.shape[0] * H,),
        out_shape=shape(local.shape, LOW),
        in_specs=[smem(), block, block],
        out_specs=block,
        compiler_params=params(60),
        cost_estimate=cost(local.size, 6 * local.size),
    )(decay, local, got)


def assemble_kernel(plan, fills, sources_of, me_ref, side_ref, *refs):
    sources, outs = refs[: len(sources_of)], refs[len(sources_of) :]
    lanes = sources[0].shape[1]
    for index, row, size in fills:
        outs[index][row : row + size, :] = jnp.zeros((size, outs[index].shape[1]), LOW)

    def place(source, lane, low, high):
        for start, index, row, size in plan:
            begin, end = max(start, low), min(start + size, high)
            if begin < end:
                to = row + begin - start
                outs[index][to : to + end - begin, pl.ds(lane, lanes)] = source[
                    begin - low : end - low, :
                ]

    for (mask, half), source in zip(sources_of, sources):
        lane = pl.multiple_of(jnp.bitwise_xor(me_ref[0], mask) * lanes, lanes)
        rows = source.shape[0]
        if half is None:
            place(source, lane, 0, rows)
            continue
        for side in range(2):

            @pl.when(side_ref[0] == side)
            def _():
                low = (side ^ half) * rows
                place(source, lane, low, low + rows)


def assemble(held, plan, fills, heights, width, me, side):
    sources_of = [(mask, half) for mask, half, part in held]
    parts = [part for mask, half, part in held]
    return pl.pallas_call(
        functools.partial(assemble_kernel, plan, fills, sources_of),
        out_shape=[shape((rows, width), LOW) for rows in heights],
        in_specs=[smem()] * 2 + [pl.BlockSpec(memory_space=VMEM)] * len(parts),
        out_specs=[pl.BlockSpec(memory_space=VMEM)] * len(heights),
        compiler_params=params(20),
        cost_estimate=cost(0, 4 * sum(heights) * width),
    )(me, side, *parts)


def rotated(flat, cosine, sine):
    half = KD // 2
    parts = []
    for h in range(H):
        u = flat[:, h * KD : h * KD + half]
        w = flat[:, h * KD + half : (h + 1) * KD]
        parts += [u * cosine - w * sine, w * cosine + u * sine]
    return jnp.concatenate(parts, axis=1)


def column(size):
    return lax.broadcasted_iota(jnp.int32, (size, 1), 0).astype(WIDE)


def front_kernel(count, decay, seg_s, tok, w, gains, cos, sin, seg, *rest):
    hid, k, v, kv, out_state, state = rest
    seq = pl.program_id(0) // count
    c = pl.program_id(0) % count
    x = tok[...].astype(WIDE)
    r = lax.rsqrt(jnp.mean(x * x, axis=1, keepdims=True) + EPS)
    h1 = (x * r * gains[0:1, :].astype(WIDE)).astype(LOW)
    hid[...] = h1
    kd = H * KD
    key = rotated(dot_nt(h1, w[kd : 2 * kd, :]), cos[...], sin[...]).astype(LOW)
    k[...] = key
    val = dot_nt(h1, w[2 * kd :, :]).astype(LOW)
    v[...] = val
    first = seg_s[seq, c * BLOCK]
    last = seg_s[seq, c * BLOCK + BLOCK - 1]
    before = seg_s[seq, jnp.maximum(c * BLOCK - 1, 0)]
    here = (seg[...] == last).astype(WIDE)
    joined = jnp.logical_and(jnp.logical_and(first == last, first == before), c > 0)
    for h in range(H):
        a = decay[h]
        kw = jnp.exp(a * (BLOCK - 1.0 - column(BLOCK))) * here
        kk = (key[:, h * KD : (h + 1) * KD].astype(WIDE) * kw).astype(LOW)
        add = dot_tn(kk, val[:, h * VP : (h + 1) * VP])
        kv[h] = add
        factor = jnp.exp(jnp.full((1, 1), a * BLOCK, WIDE))
        total = jnp.where(joined, factor * state[h], 0.0) + add
        state[h] = total
        out_state[h] = total.astype(LOW)


def row_block(width):
    return pl.BlockSpec((BLOCK, width), lambda t: (t, 0))


def state_block(count, at=lambda c: c):
    return pl.BlockSpec(
        (None, None, H, KD, VP), lambda t: (t // count, at(t % count), 0, 0, 0)
    )


def seq_block(count):
    return pl.BlockSpec((None, H, KD, VP), lambda t: (t // count, 0, 0, 0))


def front(seqs, length, tokens, seg_col, segments, decay, w, gains, cos, sin):
    count = length // BLOCK
    rows, width = tokens.shape
    outs = [width, H * KD, H * VP]
    table = pl.BlockSpec((BLOCK, KD // 2), lambda t: (t % count, 0))
    return pl.pallas_call(
        functools.partial(front_kernel, count),
        grid=(seqs * count,),
        out_shape=[shape((rows, n), LOW) for n in outs]
        + [shape((seqs, count, H, KD, VP), WIDE), shape((seqs, H, KD, VP), LOW)],
        in_specs=[smem(), smem(), row_block(width), whole(w.shape), whole(gains.shape)]
        + [table, table, row_block(1)],
        out_specs=[row_block(n) for n in outs]
        + [state_block(count), seq_block(count)],
        scratch_shapes=[VMEM((H, KD, VP), WIDE)],
        compiler_params=params(60),
        cost_estimate=cost(2 * rows * width * w.shape[0], 12 * rows * width),
    )(decay, segments, tokens, w, gains, cos, sin, seg_col)


def decay_row(a):
    return jnp.exp(-a * lax.broadcasted_iota(jnp.int32, (1, BLOCK), 1).astype(WIDE))


def mixing(a, top, size, seg, seg_row):
    reach = top + size
    rows = jnp.exp(a * (column(size) + float(top)))
    same = seg[top:reach, :] == seg_row[:, :reach]
    n = lax.broadcasted_iota(jnp.int32, (size, reach), 0) + top
    m = lax.broadcasted_iota(jnp.int32, (size, reach), 1)
    return jnp.where(jnp.logical_and(same, n >= m), rows * decay_row(a)[:, :reach], 0.0)


TILE = 256


def inner_kernel(decay, k, v, hid, w, cos, sin, seg, seg_row, q, intra):
    query = rotated(dot_nt(hid[...], w[...]), cos[...], sin[...]).astype(LOW)
    q[...] = query
    for i in range(BLOCK // TILE):
        top, reach = i * TILE, (i + 1) * TILE
        for h in range(H):
            s = dot_nt(query[top:reach, h * KD : (h + 1) * KD], k[:reach, h * KD : (h + 1) * KD])
            weights = (s * mixing(decay[h], top, TILE, seg, seg_row)).astype(LOW)
            intra[top:reach, h * VP : (h + 1) * VP] = dot(
                weights, v[:reach, h * VP : (h + 1) * VP]
            ).astype(LOW)


def inner(k, v, hid, w, cos, sin, seg_col, seg_row, decay, length):
    rows, width = hid.shape
    count = length // BLOCK
    block = lambda n: pl.BlockSpec((BLOCK, n), lambda t: (t, 0))
    table = pl.BlockSpec((BLOCK, KD // 2), lambda t: (t % count, 0))
    return pl.pallas_call(
        inner_kernel,
        grid=(rows // BLOCK,),
        out_shape=[shape((rows, n), LOW) for n in (H * KD, H * VP)],
        in_specs=[
            smem(),
            block(H * KD),
            block(H * VP),
            block(width),
            pl.BlockSpec((H * KD, width), lambda t: (0, 0)),
            table,
            table,
            block(1),
            pl.BlockSpec((None, 1, BLOCK), lambda t: (t, 0, 0)),
        ],
        out_specs=[block(n) for n in (H * KD, H * VP)],
        compiler_params=params(60),
        cost_estimate=cost(rows * (2 * width * 512 + 2 * BLOCK * H * VP), 8 * rows * H * VP),
    )(decay, k, v, hid, w, cos, sin, seg_col, seg_row)


def gate_kernel(hid, w, gate):
    gate[...] = dot_nt(hid[...], w[...]).astype(LOW)


def gates(hid, w):
    rows, width = hid.shape
    vp = H * VP
    return pl.pallas_call(
        gate_kernel,
        grid=(rows // BLOCK,),
        out_shape=shape((rows, vp), LOW),
        in_specs=[row_block(width), pl.BlockSpec((vp, width), lambda t: (0, 0))],
        out_specs=row_block(vp),
        compiler_params=params(60),
        cost_estimate=cost(2 * rows * width * vp, 4 * rows * vp),
    )(hid, w)


CHUNK = 16


def interleaved(first, second):
    steps = [((i + 0.5) / len(first), 0, step) for i, step in enumerate(first)]
    steps += [((i + 0.5) / len(second), 1, step) for i, step in enumerate(second)]
    for place, which, step in sorted(steps, key=lambda item: item[:2]):
        step()


def pieces(width, size=256):
    return [(start, min(start + size, width)) for start in range(0, width, size)]


def across(narrow, width):
    return jnp.concatenate([narrow] * (width // 128), axis=1)


def middle_kernel(count, ff, decay, seg_s, in_last, *refs):
    (intra, gate, q, tok, cot, seg, w, gains, *got, kv) = refs[:12]
    outs, scratch = refs[12:24], refs[24:]
    (tok_out, hid2, prod, dgate, dup, mixed, glow, ggate, gret, st_out, dst, leave) = outs
    (state, now, queries, factors, ret_s, norm_s, silu_s, slope_s, inv_s, res_s, ff_s, low_s, sums) = scratch
    seq = pl.program_id(0) // count
    c = pl.program_id(0) % count
    start = c * BLOCK
    vp = H * VP
    width = tok.shape[1]
    before = jnp.where(c > 0, seg_s[seq, jnp.maximum(start - 1, 0)], in_last[seq])

    @pl.when(c == 0)
    def _():
        for h in range(H):
            total = entering(decay, count * BLOCK, h, got)
            state[h] = total
            now[h] = total.astype(LOW)

    for b in range(1, count):

        @pl.when(c == b)
        def _():
            prev = seg_s[seq, (b - 1) * BLOCK - 1] if b > 1 else in_last[seq]
            joined = jnp.logical_and(
                seg_s[seq, (b - 1) * BLOCK] == seg_s[seq, b * BLOCK - 1],
                seg_s[seq, (b - 1) * BLOCK] == prev,
            )
            for h in range(H):
                factor = jnp.exp(jnp.full((1, 1), decay[h] * BLOCK, WIDE))
                total = jnp.where(joined, factor * state[h], 0.0) + kv[h]
                state[h] = total
                now[h] = total.astype(LOW)

    st_out[...] = now[...]
    here = (seg[...] == before).astype(WIDE)
    for h in range(H):
        qw = jnp.exp(decay[h] * (column(BLOCK) + 1.0)) * here
        factors[h] = jnp.broadcast_to(qw, (BLOCK, 128))

    w_out = (vp, 2 * vp)
    w_gate = (2 * vp, 2 * vp + ff)
    w_up = (2 * vp + ff, 2 * vp + 2 * ff)
    w_down = (2 * vp + 2 * ff, 2 * vp + 3 * ff)
    gain = gains[1:2, :].astype(WIDE)

    def phases(top):
        rs = pl.ds(top, TILE)
        lists = []

        def add(steps):
            lists.append(steps)

        def chunks():
            return [pl.ds(row, CHUNK) for row in range(top, top + TILE, CHUNK)]

        def cross(h, lo, hi):
            ret_s[rs, h * VP + lo : h * VP + hi] = dot(
                q[rs, h * KD : (h + 1) * KD], now[h, :, lo:hi]
            )

        add([functools.partial(cross, h, *piece) for h in range(H) for piece in pieces(VP)])

        def gated(h, r):
            hv = slice(h * VP, (h + 1) * VP)
            hk = slice(h * KD, (h + 1) * KD)
            qw = factors[h, r, :]
            queries[r, hk] = (q[r, hk].astype(WIDE) * across(qw, KD)).astype(LOW)
            ret = intra[r, hv].astype(WIDE) + across(qw, VP) * ret_s[r, hv]
            mean = jnp.sum(ret, axis=1, keepdims=True) * (1.0 / VD)
            centered = ret - mean
            square = jnp.sum(centered * centered, axis=1, keepdims=True)
            var = (square - (VP - VD) * (mean * mean)) * (1.0 / VD)
            inv = lax.rsqrt(var + 1.0 * KD)
            nh = centered * inv
            g = gate[r, hv].astype(WIDE)
            sg = 0.5 * jnp.tanh(0.5 * g) + 0.5
            sl = g * sg
            mixed[r, hv] = (nh * sl).astype(LOW)
            norm_s[r, hv] = nh
            silu_s[r, hv] = sl
            slope_s[r, hv] = nh * (sg + sl * (1.0 - sg))
            inv_s[h, r, :] = jnp.broadcast_to(inv, (CHUNK, 128))

        add([functools.partial(gated, h, r) for r in chunks() for h in range(H)])

        def project(lo, hi):
            res_s[rs, lo:hi] = dot(mixed[rs, :], w[w_out[0] : w_out[1], lo:hi])

        add([functools.partial(project, *piece) for piece in pieces(width)])

        def norm(r):
            resid = tok[r, :].astype(WIDE) + res_s[r, :]
            r2 = lax.rsqrt(jnp.mean(resid * resid, axis=1, keepdims=True) + EPS)
            res_s[r, :] = resid
            hid2[r, :] = (resid * r2 * gain).astype(LOW)
            inv_s[H, r, :] = jnp.broadcast_to(r2, (CHUNK, 128))

        add([functools.partial(norm, r) for r in chunks()])

        def forward(place, source, at, lo, hi):
            ff_s[place, rs, lo:hi] = dot_nt(source[rs, :], w[at[0] + lo : at[0] + hi, :])

        add(
            [
                functools.partial(forward, place, source, at, *piece)
                for piece in pieces(ff)
                for place, source, at in ((0, hid2, w_gate), (1, hid2, w_up), (2, cot, w_down))
            ]
        )

        def gelu(r, lo, hi):
            gf, uf, gp = ff_s[0, r, lo:hi], ff_s[1, r, lo:hi], ff_s[2, r, lo:hi]
            e = jnp.exp(-0.5 * (gf * gf))
            d = 1.0 / (1.0 + (0.3275911 * math.sqrt(0.5)) * jnp.abs(gf))
            poly = d * (
                0.5 * 0.254829592
                + d
                * (
                    0.5 * -0.284496736
                    + d * (0.5 * 1.421413741 + d * (0.5 * -1.453152027 + d * (0.5 * 1.061405429)))
                )
            )
            tail = poly * e
            cdf = jnp.where(gf >= 0.0, 1.0 - tail, tail)
            ge = gf * cdf
            dge = cdf + gf * (e * (1.0 / math.sqrt(2.0 * math.pi)))
            prod[r, lo:hi] = (ge * uf).astype(LOW)
            dgate[r, lo:hi] = (gp * uf * dge).astype(LOW)
            dup[r, lo:hi] = (gp * ge).astype(LOW)

        add([functools.partial(gelu, r, *piece) for r in chunks() for piece in pieces(ff, 512)])

        def down(lo, hi):
            low_s[0, rs, lo:hi] = dot(prod[rs, :], w[w_down[0] : w_down[1], lo:hi])

        def hidden(lo, hi):
            low_s[1, rs, lo:hi] = dot(dgate[rs, :], w[w_gate[0] : w_gate[1], lo:hi]) + dot(
                dup[rs, :], w[w_up[0] : w_up[1], lo:hi]
            )

        add([functools.partial(step, *piece) for piece in pieces(width) for step in (down, hidden)])

        def residual(r):
            resid = res_s[r, :]
            r2 = across(inv_s[H, r, :], width)
            tok_out[r, :] = (resid + low_s[0, r, :]).astype(LOW)
            gh = low_s[1, r, :] * gain
            xhat = resid * r2
            inner_product = jnp.mean(gh * xhat, axis=1, keepdims=True)
            glow[r, :] = (cot[r, :].astype(WIDE) + r2 * (gh - xhat * inner_product)).astype(LOW)

        add([functools.partial(residual, r) for r in chunks()])

        def mix_back(lo, hi):
            ret_s[rs, lo:hi] = dot_nt(glow[rs, :], w[w_out[0] + lo : w_out[0] + hi, :])

        add([functools.partial(mix_back, *piece) for piece in pieces(vp)])

        def gated_back(h, r):
            hv = slice(h * VP, (h + 1) * VP)
            gm = ret_s[r, hv]
            nh = norm_s[r, hv]
            ggate[r, hv] = (gm * slope_s[r, hv]).astype(LOW)
            gn = gm * silu_s[r, hv]
            one = jnp.sum(gn, axis=1, keepdims=True) * (1.0 / VD)
            two = jnp.sum(gn * nh, axis=1, keepdims=True) * (1.0 / VD)
            gret[r, hv] = (across(inv_s[h, r, :], VP) * (gn - one - nh * two)).astype(LOW)

        add([functools.partial(gated_back, h, r) for r in chunks() for h in range(H)])
        return lists

    first, second = phases(0), phases(TILE)
    for k in range(len(first) + 1):
        interleaved(first[k] if k < len(first) else [], second[k - 1] if k else [])
    for h in range(H):
        add = dot_tn(queries[:, h * KD : (h + 1) * KD], gret[:, h * VP : (h + 1) * VP])
        dst[h] = add
        sums[c, h] = add

    @pl.when(c == count - 1)
    def _():
        for h in range(H):
            total = sums[count - 1, h]
            for b in reversed(range(count - 1)):
                prev = seg_s[seq, b * BLOCK - 1] if b > 0 else in_last[seq]
                joined = jnp.logical_and(
                    seg_s[seq, b * BLOCK] == seg_s[seq, (b + 1) * BLOCK - 1],
                    seg_s[seq, b * BLOCK] == prev,
                )
                factor = jnp.exp(jnp.full((1, 1), decay[h] * BLOCK, WIDE))
                total = jnp.where(joined, factor * total, 0.0) + sums[b, h]
            leave[h] = total.astype(LOW)


def middle(seqs, length, ff, data, seg_col, segments, in_last, decay, w, gains, got, kv):
    intra, gate, q, tokens, cotangent = data
    rows, width = tokens.shape
    count = length // BLOCK
    vp = H * VP
    outs = [width, width, ff, ff, ff, vp, width, vp, vp]
    inputs = [decay, segments, in_last, intra, gate, q, tokens, cotangent, seg_col, w, gains, *got, kv]
    specs = [smem()] * 3 + [row_block(n) for n in (vp, vp, H * KD, width, width, 1)]
    specs += [whole(w.shape), whole(gains.shape), *[seq_block(count)] * 3]
    specs += [state_block(count, lambda c: jnp.maximum(c - 1, 0))]
    one = (H, KD, VP)
    states = (seqs, count, *one)
    return pl.pallas_call(
        functools.partial(middle_kernel, count, ff),
        grid=(seqs * count,),
        out_shape=[shape((rows, n), LOW) for n in outs]
        + [shape(states, LOW), shape(states, WIDE), shape((seqs, *one), LOW)],
        in_specs=specs,
        out_specs=[row_block(n) for n in outs]
        + [state_block(count)] * 2
        + [seq_block(count)],
        scratch_shapes=[
            VMEM(one, WIDE),
            VMEM(one, LOW),
            VMEM((BLOCK, H * KD), LOW),
            VMEM((H, BLOCK, 128), WIDE),
            VMEM((BLOCK, vp), WIDE),
            VMEM((BLOCK, vp), WIDE),
            VMEM((BLOCK, vp), WIDE),
            VMEM((BLOCK, vp), WIDE),
            VMEM((H + 1, BLOCK, 128), WIDE),
            VMEM((BLOCK, width), WIDE),
            VMEM((3, BLOCK, ff), WIDE),
            VMEM((2, BLOCK, width), WIDE),
            VMEM(states[1:], WIDE),
        ],
        compiler_params=params(60),
        cost_estimate=cost(2 * rows * width * (2 * vp + 6 * ff), 30 * rows * width),
    )(*inputs)


def weight_kernel(plan, count, layout, me_ref, *refs):
    ins, ready, outs, total = refs[:count], refs[count:-3], refs[-3:-1], refs[-1]
    if layout is None:
        outs = refs[-2:-1]
    t = pl.program_id(0)
    last = pl.num_programs(0) - 1
    for left, right, cuts in plan:
        a, b = ins[left], ins[right]
        for source, row, size in cuts:
            add = dot_tn(a[:, source : source + size], b[...])

            @pl.when(t == 0)
            def _():
                total[row : row + size, :] = add

            @pl.when(t > 0)
            def _():
                total[row : row + size, :] += add

    @pl.when(t == last)
    def _():
        used = max(row + size for left, right, cuts in plan for source, row, size in cuts)
        if layout is None:
            outs[0][...] = total[...].astype(LOW)
            return
        for item in ready:
            total[used : used + item.shape[0], :] = item[...].astype(WIDE)
            used += item.shape[0]
        if used < total.shape[0]:
            total[used:, :] = jnp.zeros((total.shape[0] - used, total.shape[1]), WIDE)
        lanes = outs[0].shape[2]
        which, pieces = layout
        rows = outs[0].shape[1] // pieces
        for part in range(2 * outs[0].shape[0]):
            target = outs[part & 1]
            lane = pl.multiple_of(jnp.bitwise_xor(me_ref[0], part) * lanes, lanes)
            for q in range(pieces):
                row = pl.multiple_of(jnp.bitwise_xor(me_ref[which], q) * rows, 16)
                target[part >> 1, q * rows : (q + 1) * rows, :] = total[
                    pl.ds(row, rows), pl.ds(lane, lanes)
                ].astype(LOW)


def weight_grads(arrays, plan, place, shards=2, height=0, layout=None, ready=()):
    rows = arrays[0].shape[0]
    used = max(row + size for left, right, cuts in plan for source, row, size in cuts)
    width = arrays[plan[0][1]].shape[1]
    tile = 2 * BLOCK
    block = lambda n: pl.BlockSpec((tile, n), lambda t: (t, 0))
    dims = [(shards // 2, height, width // shards)] * 2
    if layout is None:
        height, dims = used, [(used, width)]
    full = lambda item: pl.BlockSpec(item, lambda t: (0,) * len(item))
    return pl.pallas_call(
        functools.partial(weight_kernel, plan, len(arrays), layout),
        grid=(rows // tile,),
        out_shape=[shape(item, LOW) for item in dims],
        in_specs=[smem()] + [block(item.shape[1]) for item in arrays]
        + [full(item.shape) for item in ready],
        out_specs=[full(item) for item in dims],
        scratch_shapes=[VMEM((height, width), WIDE)],
        compiler_params=params(60),
        cost_estimate=cost(2 * rows * used * width, 2 * rows * sum(i.shape[1] for i in arrays)),
    )(place, *arrays, *ready)


def back_kernel(count, decay, seg_s, in_last, *refs):
    (q, k, v, gret, cos, sin, seg, seg_row, st, dst, *got) = refs[:13]
    (dq, dk, dv, state, weights, grads) = refs[13:]
    seq = pl.program_id(0) // count
    c = count - 1 - pl.program_id(0) % count

    @pl.when(c == count - 1)
    def _():
        for h in range(H):
            state[h] = entering(decay, count * BLOCK, h, got)

    for b in range(1, count):

        @pl.when(c == b - 1)
        def _():
            prev = seg_s[seq, b * BLOCK - 1]
            first = seg_s[seq, b * BLOCK]
            last = seg_s[seq, (b + 1) * BLOCK - 1]
            joined = jnp.logical_and(first == last, first == prev)
            for h in range(H):
                factor = jnp.exp(jnp.full((1, 1), decay[h] * BLOCK, WIDE))
                state[h] = jnp.where(joined, factor * state[h], 0.0) + dst[h]

    start = c * BLOCK
    before = jnp.where(c > 0, seg_s[seq, jnp.maximum(start - 1, 0)], in_last[seq])
    final = seg_s[seq, start + BLOCK - 1]
    here = (seg[...] == before).astype(WIDE)
    ends = (seg[...] == final).astype(WIDE)
    place = column(BLOCK)
    dqs, dks = [], []
    for h in range(H):
        a = decay[h]
        qh = q[:, h * KD : (h + 1) * KD]
        kh = k[:, h * KD : (h + 1) * KD]
        vh = v[:, h * VP : (h + 1) * VP]
        gh = gret[:, h * VP : (h + 1) * VP]
        qw = jnp.exp(a * (place + 1.0)) * here
        kw = jnp.exp(a * (BLOCK - 1.0 - place)) * ends
        parts = []
        for i in range(BLOCK // TILE):
            top, reach = i * TILE, (i + 1) * TILE
            mix = mixing(a, top, TILE, seg, seg_row)
            s = dot_nt(qh[top:reach, :], kh[:reach, :])
            weights[top:reach, :reach] = (s * mix).astype(LOW)
            gs = (dot_nt(gh[top:reach, :], vh[:reach, :]) * mix).astype(LOW)
            grads[top:reach, :reach] = gs
            parts.append(dot(gs, kh[:reach, :]))
        late = state[h].astype(LOW)
        dqs.append(jnp.concatenate(parts) + qw * dot_nt(gh, st[h]))
        parts, values = [], []
        for i in range(BLOCK // TILE):
            top, reach = i * TILE, (i + 1) * TILE
            parts.append(dot_tn(grads[top:, top:reach], qh[top:, :]))
            values.append(dot_tn(weights[top:, top:reach], gh[top:, :]))
        dks.append(jnp.concatenate(parts) + kw * dot_nt(vh, late))
        dv[:, h * VP : (h + 1) * VP] = (jnp.concatenate(values) + kw * dot(kh, late)).astype(LOW)
    dq[...] = rotated(jnp.concatenate(dqs, axis=1), cos[...], -sin[...]).astype(LOW)
    dk[...] = rotated(jnp.concatenate(dks, axis=1), cos[...], -sin[...]).astype(LOW)


def back(seqs, length, data, cos, sin, seg_col, seg_row, segments, in_last, decay, st, dst, got):
    rows = data[0].shape[0]
    count = length // BLOCK
    turn = lambda t: (t // count) * count + count - 1 - t % count
    block = lambda n: pl.BlockSpec((BLOCK, n), lambda t: (turn(t), 0))
    table = pl.BlockSpec((BLOCK, KD // 2), lambda t: (count - 1 - t % count, 0))
    outs = [H * KD, H * KD, H * VP]
    inputs = [decay, segments, in_last, *data, cos, sin, seg_col, seg_row, st, dst, *got]
    specs = [smem()] * 3 + [block(item.shape[1]) for item in data] + [table, table, block(1)]
    specs += [pl.BlockSpec((None, 1, BLOCK), lambda t: (turn(t), 0, 0))]
    specs += [state_block(count, lambda c: count - 1 - c)]
    specs += [state_block(count, lambda c: jnp.minimum(count - c, count - 1))]
    specs += [seq_block(count)] * 3
    return pl.pallas_call(
        functools.partial(back_kernel, count),
        grid=(seqs * count,),
        out_shape=[shape((rows, n), LOW) for n in outs],
        in_specs=specs,
        out_specs=[block(n) for n in outs],
        scratch_shapes=[
            VMEM((H, KD, VP), WIDE),
            VMEM((BLOCK, BLOCK), LOW),
            VMEM((BLOCK, BLOCK), LOW),
        ],
        compiler_params=params(60),
        cost_estimate=cost(rows * H * 2 * BLOCK * 3 * (KD + VP), 16 * rows * H * VP),
    )(*inputs)


def input_kernel(dq, dk, dv, ggate, tok, glow, w, w_gate, gains, *rest):
    out = rest[-1]
    kd = H * KD
    gh = dot(dq[...], w[:kd, :]) + dot(dk[...], w[kd : 2 * kd, :])
    gh += dot(dv[...], w[2 * kd :, :]) + dot(ggate[...], w_gate[...])
    x = tok[...].astype(WIDE)
    r = lax.rsqrt(jnp.mean(x * x, axis=1, keepdims=True) + EPS)
    xhat = x * r
    gh = gh * gains[0:1, :].astype(WIDE)
    inner_product = jnp.mean(gh * xhat, axis=1, keepdims=True)
    out[...] = (glow[...].astype(WIDE) + r * (gh - xhat * inner_product)).astype(LOW)


def input_grad(first, steps, dq, dk, dv, ggate, tokens, glow, w, w_rest, gains, earlier):
    rows, width = tokens.shape
    parts = rows // BLOCK // steps
    arrays = [dq, dk, dv, ggate, tokens, glow]
    block = lambda item: pl.BlockSpec((BLOCK, item.shape[1]), lambda t: (first + t, 0))
    inputs = [*arrays, w, w_rest, gains]
    specs = [block(item) for item in arrays] + [whole(w.shape)]
    specs += [pl.BlockSpec((H * VP, width), lambda t: (0, 0)), whole(gains.shape)]
    aliases = {}
    if earlier is not None:
        aliases = {len(inputs): 0}
        inputs.append(earlier)
        specs.append(pl.BlockSpec(memory_space=pl.ANY))
    return pl.pallas_call(
        input_kernel,
        grid=(steps,),
        out_shape=shape((rows, width), LOW),
        in_specs=specs,
        out_specs=block(tokens),
        input_output_aliases=aliases,
        compiler_params=params(32),
        cost_estimate=cost(2 * rows * width * (w.shape[0] + H * VP) // parts, 20 * rows * width // parts),
    )(*inputs)


def adam_step(master, moment, second, grad, scale, rate, decay_weight):
    clipped = grad * scale
    moment_new = BETA_ONE * moment + (1.0 - BETA_ONE) * clipped
    second_new = BETA_TWO * second + (1.0 - BETA_TWO) * clipped * clipped
    corrected = (
        moment_new
        * (1.0 / (1.0 - BETA_ONE**STEP))
        / (jnp.sqrt(second_new * (1.0 / (1.0 - BETA_TWO**STEP))) + ADAM_EPS)
    )
    return (master - rate * (corrected + decay_weight * master), moment_new, second_new)


def squares_kernel(vd, ff, layouts, place, *refs):
    halves, (w_qk, w_vg, w_gu, low_gains) = refs[:4], refs[4:8]
    grad_gains, total, early, late = refs[8:]
    kd = H * KD
    for index, target in enumerate((early, late)):
        which, pieces = layouts[index]
        rows = target.shape[0] // pieces
        for q in range(pieces):
            row = pl.multiple_of(jnp.bitwise_xor(place[which], q) * rows, 16)
            source = halves[2 * index + q // (pieces // 2)]
            start = q % (pieces // 2) * rows
            target[pl.ds(row, rows), :] = source[start : start + rows, :]

    def rows(source, start, size):
        return source[start : start + size, :].astype(WIDE)

    def product(weight, grad):
        return jnp.sum(weight.astype(LOW).astype(WIDE) * grad, axis=0, keepdims=True)

    sums = []

    def square(item):
        sums.append(jnp.sum(item * item, axis=0, keepdims=True))
        return item

    first = jnp.zeros((1, low_gains.shape[1]), WIDE)
    for i in range(2):
        grad = square(rows(late, i * kd, kd))
        first += jnp.sum(w_qk[i].astype(LOW).astype(WIDE).T * grad, axis=0, keepdims=True)
    first += product(w_vg[0], square(rows(late, 2 * kd, vd)))
    first += product(w_vg[1], square(rows(early, vd, vd)))
    square(rows(early, 0, vd))
    square(rows(early, 2 * vd, ff))
    second = product(w_gu[0], square(rows(early, 2 * vd + ff, ff)))
    second += product(w_gu[1], square(rows(early, 2 * vd + 2 * ff, ff)))
    gains = jnp.concatenate([first, second]) / low_gains[...].astype(LOW).astype(WIDE)
    grad_gains[...] = gains
    sums.append(jnp.sum(gains * gains, axis=0, keepdims=True))
    total[...] = jnp.broadcast_to(jnp.sum(sum(sums), axis=1, keepdims=True), total.shape)


def squares(vd, ff, layouts, place, grads, w_qk, w_vg, w_gu, gains):
    halves = [half for pair in grads for half in pair]
    vmem = pl.BlockSpec(memory_space=VMEM)
    return pl.pallas_call(
        functools.partial(squares_kernel, vd, ff, layouts),
        out_shape=[shape(gains.shape, WIDE), shape((8, 128), WIDE)]
        + [shape((2 * pair[0].shape[0], pair[0].shape[1]), LOW) for pair in grads],
        in_specs=[smem()] + [vmem] * 8,
        out_specs=[vmem] * 4,
        compiler_params=params(20),
    )(place, *halves, w_qk, w_vg, w_gu, gains)


def update_kernel(vd, ff, *refs):
    totals, (early, late, gain_grads) = refs[:4], refs[4:7]
    sources, targets, norm_out = refs[7:25], refs[25:43], refs[43]
    ins, outs = refs[44:62], refs[62:80]
    arrived, sent = refs[80:]
    kd = H * KD
    order = [4, 3, 2, 1, 0, 5]
    places = [6 * group + place for place in order for group in range(3)]
    fetch = {i: pltpu.make_async_copy(sources[i], ins[i], arrived.at[i]) for i in places}
    send = {i: pltpu.make_async_copy(outs[i], targets[i], sent.at[i]) for i in places}
    for i in places:
        fetch[i].start()
    norm = jnp.sqrt((totals[0][...] + totals[1][...]) + (totals[2][...] + totals[3][...]))
    norm_out[0, 0] = jnp.max(norm)
    scale = jnp.minimum(1.0, CLIP / (norm + 1e-06))[0:1, 0:1]

    def step(place, at, grad, rate, decay_weight):
        results = adam_step(
            ins[place][at], ins[6 + place][at], ins[12 + place][at], grad, scale, rate, decay_weight
        )
        for group, result in enumerate(results):
            outs[6 * group + place][at] = result

    def rows(source, start, size):
        return source[start : start + size, :].astype(WIDE)

    grads = {
        4: [(..., lambda: rows(early, 2 * vd, ff))],
        3: [(i, lambda i=i: rows(early, 2 * vd + (1 + i) * ff, ff)) for i in range(2)],
        2: [(..., lambda: rows(early, 0, vd))],
        1: [(0, lambda: rows(late, 2 * kd, vd)), (1, lambda: rows(early, vd, vd))],
        0: [(i, lambda i=i: rows(late, i * kd, kd).T) for i in range(2)],
        5: [(..., lambda: gain_grads[...])],
    }
    for place in order:
        for group in range(3):
            fetch[6 * group + place].wait()
        rate, decay_weight = (GAIN_RATE, 0.0) if place == 5 else (MATRIX_RATE, DECAY_WEIGHT)
        for at, grad in grads[place]:
            step(place, at, grad(), rate, decay_weight)
        for group in range(3):
            send[6 * group + place].start()
    for i in places:
        send[i].wait()


def update(vd, ff, totals, grads, gain_grads, arrays):
    anywhere = pl.BlockSpec(memory_space=pl.ANY)
    return pl.pallas_call(
        functools.partial(update_kernel, vd, ff),
        out_shape=[shape(item.shape, WIDE) for item in arrays] + [shape((1, 1), WIDE)],
        in_specs=[pl.BlockSpec(memory_space=VMEM)] * 7 + [anywhere] * 18,
        out_specs=[anywhere] * 18 + [smem()],
        scratch_shapes=[VMEM(item.shape, WIDE) for item in arrays] * 2
        + [pltpu.SemaphoreType.DMA((18,))] * 2,
        compiler_params=params(40),
    )(*totals, *grads, gain_grads, *arrays)


def on_device(
    tokens,
    cotangent,
    segments,
    log_decay,
    w_qk,
    w_vg,
    w_out,
    w_gu,
    w_down,
    norm_gains,
    *states,
):
    turned = lambda item: jnp.swapaxes(item, 1, 2)
    shards = lax.axis_size("shard")
    me = lax.axis_index("shard").reshape(1)
    replica = lax.axis_index("dp")
    count = bits_of("dp")
    halved = (tuple(range(count)), (1,))
    numbers = [
        sum(((replica >> bit) & 1) << (len(bits) - 1 - i) for i, bit in enumerate(bits))
        for bits in halved
    ]
    layouts = [(1 + i, 2 ** len(bits)) for i, bits in enumerate(halved)]
    place = jnp.concatenate([me, jnp.stack(numbers)])
    seqs, length, width = tokens.shape
    rows = seqs * length
    kd, vd, ff = H * KD, H * VD, w_down.shape[0]
    vp = H * VP
    vg_t, gu_t = turned(w_vg), turned(w_gu)

    low = lambda item: item.astype(LOW)
    def heads(item):
        return [
            jnp.pad(item[h * VD : (h + 1) * VD], ((0, VP - VD), (0, 0))) for h in range(H)
        ]

    first = jnp.concatenate(
        [
            low(w_qk[0]).T,
            low(w_qk[1]).T,
            low(vg_t[0]),
            jnp.pad(low(norm_gains), ((0, 14), (0, 0))),
        ]
    )
    rest = jnp.concatenate(
        [*heads(low(vg_t[1])), *heads(low(w_out)), low(gu_t[0]), low(gu_t[1]), low(w_down)]
    )
    first_held = gather_shards(first)
    rest = after(rest, first_held[1][2])
    w_rest = lax.all_gather(rest, "shard", axis=1, tiled=True)
    side = (lax.axis_index("dp") & 1).reshape(1)

    half_width = KD // 2
    freq_rates = jnp.exp(-math.log(10000.0) * jnp.arange(half_width).astype(WIDE) / half_width)
    positions = (lax.axis_index("shard") * length + jnp.arange(length)).astype(WIDE)
    angles = positions[:, None] * freq_rates[None, :]
    cos, sin = jnp.cos(angles), jnp.sin(angles)

    tok = tokens.reshape(rows, width)
    cot = cotangent.reshape(rows, width)
    seg_col = segments.reshape(rows, 1)
    seg_row = segments.reshape(rows // BLOCK, 1, BLOCK)
    in_last = jnp.where(lax.axis_index("shard") > 0, segments[:, 0], -1)
    decay = log_decay

    def tick(*done):
        nonlocal decay, place, gains
        decay, place, gains = lax.optimization_barrier((decay, place, gains, *done))[:3]

    plan = [(0, 0, 0, 2 * kd)] + [(2 * kd + h * VD, 0, 2 * kd + h * VP, VD) for h in range(H)]
    plan += [(2 * kd + vd, 1, 0, 16)]
    fills = [(0, 2 * kd + h * VP + VD, VP - VD) for h in range(H)]
    w_qkv, gains = assemble(first_held, plan, fills, [2 * kd + vp, 16], width, me, side)
    tick(rest)
    hid, k, v, kv, leaving = front(
        seqs, length, tok, seg_col, segments, decay, w_qkv, gains, cos, sin
    )
    passing = Passing(leaving, False)
    tick(leaving)
    tick(passing.turn(decay, length, leaving))
    q, intra = inner(k, v, hid, w_qkv, cos, sin, seg_col, seg_row, decay, length)
    tick(q)
    passing.finish(q)
    gate = gates(after(hid, passing.got[1], q), w_rest)
    tick(gate)
    tokens_out, hid2, prod, dgate, dup, mixed, glow, ggate, gret, st, dst, leaving = middle(
        seqs, length, ff, (intra, gate, q, tok, cot), seg_col, segments, in_last, decay,
        w_rest, gains, passing.got, kv,
    )
    returning = Passing(leaving, True)
    tick(leaving)

    def halves(row):
        return [(h * VP, row + h * VD, VD) for h in range(H)]

    fit = lambda used, layout: used + -used % (16 * layout[1])
    plan = [(0, 1, [(0, 0, ff)]), (2, 3, [(0, ff, ff)]), (4, 3, [(0, 2 * ff, ff)])]
    (made,) = weight_grads([prod, cot, dgate, hid2, dup], plan, place)
    tick(made)
    tick(returning.turn(decay, length, made))
    plan = [(0, 1, halves(0)), (2, 3, halves(vd))]
    made = weight_grads(
        [mixed, glow, ggate, hid], plan, place, shards,
        fit(2 * vd + 3 * ff, layouts[0]), layouts[0], (made,),
    )
    tick(made[0])
    returning.finish(made[0])
    early = Reduction(made[0], after(made[1], returning.got[1]), halved[0])
    tick(early.cross(made[0]))
    dq, dk, dv = back(
        seqs, length, (q, k, v, gret), cos, sin, seg_col, seg_row, segments, in_last, decay,
        st, dst, returning.got,
    )
    tick(dq)
    tick(early.next(dq))
    plan = [(0, 3, [(0, 0, kd)]), (1, 3, [(0, kd, kd)]), (2, 3, halves(2 * kd))]
    made = weight_grads(
        [dq, dk, dv, hid], plan, place, shards, fit(2 * kd + vd, layouts[1]), layouts[1]
    )
    late = Reduction(*made, halved[1])
    tick(made[0])
    tick(early.next(made[0]))
    tick(late.cross(made[0]))
    blocks = rows // BLOCK
    data = (dq, dk, dv, ggate, tok, glow, w_qkv, w_rest)
    grad_input = None
    for part in range(2):
        grad_input = input_grad(part * blocks // 2, blocks // 2, *data, gains, grad_input)
        tick(grad_input)
        tick(late.next(grad_input), early.next(grad_input))
    while early.left() or late.left():
        for item in (early, late):
            if item.left():
                item.next()

    gain_grads, total, *grads = squares(
        vd, ff, layouts, place, [early.result(), late.result()], w_qk, vg_t, gu_t, norm_gains
    )
    others = [
        lax.ppermute(total, "shard", [(i, i ^ mask) for i in range(shards)]) for mask in (1, 2, 3)
    ]
    arrays = []
    for group in ((w_qk, w_vg, w_out, w_gu, w_down, norm_gains), states[:6], states[6:]):
        arrays += [turned(item) if i in (1, 3) else item for i, item in enumerate(group)]
    *results, norm = update(vd, ff, [total, *others], grads, gain_grads, arrays)
    results = [turned(item) if i % 6 in (1, 3) else item for i, item in enumerate(results)]
    return (
        tokens_out.reshape(tokens.shape),
        grad_input.reshape(tokens.shape),
        *results,
        norm.reshape(()),
    )


def solution(mesh):
    split = P("dp", "shard", None)
    rows, columns = P(None, "shard", None), P(None, "shard")
    group = (rows, rows, columns, rows, columns, columns)
    in_specs = (split, split, P("dp", "shard"), P()) + group * 3
    out_specs = (split, split) + group * 3 + (P(),)
    return jax.shard_map(
        on_device, mesh=mesh, in_specs=in_specs, out_specs=out_specs, check_vma=False
    )
```

profile of v0, /device:TPU:0, one launch (start us, length us, event | category | flops | bytes accessed | tf_op | source)
XLA Modules:
  0.0 294.9 jit_solution(13972327416410383188)
XLA Ops:
  9.4 3.0 %collective-permute-start = (bf16[1904,128]{1,0:T(8,128)(2,1)S(1)}, bf16[1904,128]{1,0:T(8,128)(2,1)S(1)}, u32[]{:S(2)}, u32[]{:S(2)}) collective-permute-start(bf16[1904,128]{1,0:T(8,128)(2,1)S(1)} %fusion.5.refs_0_), channel_id=1, source_target_pairs={{0,2},{1,3},{2,0},{3,1},{4,6},{5,7},{6,4},{7,5},{8,10},{9,11},{10,... | collective-permute-start | bytes 1462280 | tf_op jit(solution)/shard_map/ppermute | solution.py:72
  17.6 5.9 %collective-permute-done.refs_1_ = bf16[1904,128]{1,0:T(8,128)(2,1)S(1)} collective-permute-done((bf16[1904,128]{1,0:T(8,128)(2,1)S(1)}, bf16[1904,128]{1,0:T(8,128)(2,1)S(1)}, u32[]{:S(2)}, u32[]{:S(2)}) %collective-permute-start) | collective-permute-done | bytes 487456 | tf_op jit(solution)/shard_map/ppermute | solution.py:72
  26.1 3.0 %multiply_sine_fusion = (f32[1024,128]{1,0:T(8,128)}, f32[1024,128]{1,0:T(8,128)}) fusion(f32[128]{0:T(128)S(1)} %multiply_exponential_fusion, f32[1024]{0:T(1024)S(1)} %add_convert_fusion.11), kind=kLoop, calls=%fused_computation.11 | loop fusion | flops 131072 | bytes 1053184 | tf_op jit(solution)/shard_map/sin | solution.py:1004
  32.6 10.8 %shard_map.374 = (bf16[2048,512]{1,0:T(8,128)(2,1)}, bf16[2048,512]{1,0:T(8,128)(2,1)}, bf16[2048,1024]{1,0:T(8,128)(2,1)}, f32[2,2,2,256,512]{4,3,2,1,0:T(8,128)}, bf16[2,2,256,512]{3,2,1,0:T(8,128)(2,1)}) custom-call(f32[2]{0:T(128)} %decay.5, s32[2,1024]{1,0:T(2,128)} %seg_s.5, bf16[2048,512]{1,0:T(8,128)(2,1)} %bitcast.69, bf16[2048,512]{1,0:T(8,128)(2,1)} %copy-done.1, ...), custom_call_target="tpu_custom_call" | custom-call | flops 4294967296 | bytes 12582912 | tf_op jit(solution)/shard_map/pallas_call | solution.py:287
  45.6 2.4 collective-permute-done.3.got.refs_8_
  49.0 3.7 %shard_map.375 = bf16[2,2,256,512]{3,2,1,0:T(8,128)(2,1)} custom-call(f32[2]{0:T(128)} %decay.5, bf16[2,2,256,512]{3,2,1,0:T(8,128)(2,1)} %get-tuple-element.139.local, bf16[2,2,256,512]{3,2,1,0:T(8,128)(2,1)} %copy-done.34), custom_call_target="tpu_custom_call" | custom-call | flops 524288 | bytes 3145728 | tf_op jit(solution)/shard_map/pallas_call | solution.py:171
  54.0 10.4 %shard_map.376 = (bf16[2048,512]{1,0:T(8,128)(2,1)}, bf16[2048,1024]{1,0:T(8,128)(2,1)}) custom-call(f32[2]{0:T(128)} %decay.5, bf16[2048,512]{1,0:T(8,128)(2,1)} %get-tuple-element.147.k.refs_1_, bf16[2048,1024]{1,0:T(8,128)(2,1)} %get-tuple-element.148.v.refs_2_, bf16[2048,512]{1,0:T(8,128)(2,1)} %get-tuple-element.154.hid.refs_3_, ...), custom_call_target="tpu_custom_call" | custom-call | flops 3221225472 | bytes 16777216 | tf_op jit(solution)/shard_map/pallas_call | solution.py:336
  64.4 2.1 collective-permute-start.5
  67.2 6.1 %shard_map.377.refs_1_ = bf16[2048,1024]{1,0:T(8,128)(2,1)} custom-call(bf16[2048,512]{1,0:T(8,128)(2,1)} %get-tuple-element.154.hid.refs_3_, bf16[4640,512]{1,0:T(8,128)(2,1)} %all-gather.2.cloned.1.call-done.w.refs_6_.w_gate), custom_call_target="tpu_custom_call" | custom-call | flops 2147483648 | bytes 8388608 | tf_op jit(solution)/shard_map/pallas_call | solution.py:364
  73.2 41.8 %shard_map.378 = (bf16[2048,512]{1,0:T(8,128)(2,1)}, bf16[2048,512]{1,0:T(8,128)(2,1)}, bf16[2048,864]{1,0:T(8,128)(2,1)}, bf16[2048,864]{1,0:T(8,128)(2,1)}, bf...) custom-call(f32[2]{0:T(128)} %decay.5, ...), custom_call_target="tpu_custom_call" | custom-call | flops 15166603264 | bytes 31457280 | tf_op jit(solution)/shard_map/pallas_call | solution.py:600
  116.5 12.5 %shard_map.379.refs_4_ = bf16[2592,512]{1,0:T(8,128)(2,1)} custom-call(s32[3]{0:T(128)} %pad_add_fusion.me_ref.place, bf16[2048,864]{1,0:T(8,128)(2,1)} %get-tuple-element.166.refs_0_, bf16[2048,512]{1,0:T(8,128)(2,1)} %bitcast.89, bf16[2048,864]{1,0:T(8,128)(2,1)} %get-tuple-element.167.refs_2_, bf16[2048,512]{1,0:T(8,128)(2,1)} %get-tuple-element.168.refs_3_, ...), custom_call_target="tpu_custom_call" | custom-call | flops 5435817984 | bytes 14811136 | tf_op jit(solution)/shard_map/pallas_call | solution.py:682
  129.9 3.7 %shard_map.380 = bf16[2,2,256,512]{3,2,1,0:T(8,128)(2,1)} custom-call(f32[2]{0:T(128)} %decay.5, bf16[2,2,256,512]{3,2,1,0:T(8,128)(2,1)} %get-tuple-element.162.local, bf16[2,2,256,512]{3,2,1,0:T(8,128)(2,1)} %copy-done.33), custom_call_target="tpu_custom_call" | custom-call | flops 524288 | bytes 3145728 | tf_op jit(solution)/shard_map/pallas_call | solution.py:171
  134.3 13.9 %shard_map.381 = (bf16[2,4352,128]{2,1,0:T(8,128)(2,1)}, bf16[2,4352,128]{2,1,0:T(8,128)(2,1)}) custom-call(s32[3]{0:T(128)} %pad_add_fusion.me_ref.place, bf16[2048,1024]{1,0:T(8,128)(2,1)} %get-tuple-element.177.refs_0_, bf16[2048,512]{1,0:T(8,128)(2,1)} %get-tuple-element.178.refs_1_.glow, bf16[2048,1024]{1,0:T(8,128)(2,1)} %get-tuple-element.179.refs_2_.ggate, ...), custom_call_target="tpu_custom_call" | custom-call | flops 3623878656 | bytes 12582912 | tf_op jit(solution)/shard_map/pallas_call | solution.py:682
  148.2 8.5 %collective-permute-start.8 = (bf16[2,4352,128]{2,1,0:T(8,128)(2,1)}, bf16[2,4352,128]{2,1,0:T(8,128)(2,1)S(1)}, u32[]{:S(2)}, u32[]{:S(2)}) collective-permute-start(bf16[2,4352,128]{2,1,0:T(8,128)(2,1)} %get-tuple-element.185), channel_id=1, source_target_pairs={{0,1},{1,0},{2,3},{3,2},{4,5},{5,4},{6,7},{7,6},{8,9},{9,8},{10,11... | collective-permute-start | bytes 6684680 | tf_op jit(solution)/shard_map/ppermute | solution.py:72
  158.2 2.7 collective-permute-done.8
  160.9 3.3 %fusion = bf16[4352,128]{1,0:T(8,128)(2,1)} fusion(bf16[2,4352,128]{2,1,0:T(8,128)(2,1)S(1)} %collective-permute-done.8, bf16[2,4352,128]{2,1,0:T(8,128)(2,1)} %get-tuple-element.180), kind=kLoop, calls=%fused_computation.1 | loop fusion | flops 2228224 | bytes 3342336 | tf_op jit(solution)/shard_map/convert_element_type | solution.py:83
  167.0 18.1 %shard_map.382 = (bf16[2048,512]{1,0:T(8,128)(2,1)}, bf16[2048,512]{1,0:T(8,128)(2,1)}, bf16[2048,1024]{1,0:T(8,128)(2,1)}) custom-call(f32[2]{0:T(128)} %decay.5, s32[2,1024]{1,0:T(2,128)} %seg_s.5, s32[2]{0:T(128)} %select_reduce_fusion.in_last, bf16[2048,512]{1,0:T(8,128)(2,1)} %get-tuple-element.150.refs_2_.refs_0_, ...), custom_call_target="tpu_custom_call" | custom-call | flops 9663676416 | bytes 33554432 | tf_op jit(solution)/shard_map/pallas_call | solution.py:768
  185.1 6.3 %collective-permute-done.10 = bf16[4352,128]{1,0:T(8,128)(2,1)} collective-permute-done((bf16[4352,128]{1,0:T(8,128)(2,1)}, bf16[4352,128]{1,0:T(8,128)(2,1)}, u32[]{:S(2)}, u32[]{:S(2)}) %collective-permute-start.10) | collective-permute-done | bytes 1114144 | tf_op jit(solution)/shard_map/ppermute | solution.py:72
  191.4 3.0 %fusion.1 = (bf16[2176,128]{1,0:T(8,128)(2,1)}, bf16[2176,128]{1,0:T(8,128)(2,1)}) fusion(bf16[4352,128]{1,0:T(8,128)(2,1)} %collective-permute-done.10, bf16[2,4352,128]{2,1,0:T(8,128)(2,1)} %copy-done.32, bf16[2,4352,128]{2,1,0:T(8,128)(2,1)S(1)} %copy-done.31), kind=kLoop, calls=%fused_computation.3 | loop fusion | flops 3342336 | bytes 4456448 | tf_op jit(solution)/shard_map/convert_element_type | solution.py:106
  196.1 10.6 %shard_map.383 = (bf16[2,1888,128]{2,1,0:T(8,128)(2,1)}, bf16[2,1888,128]{2,1,0:T(8,128)(2,1)}) custom-call(s32[3]{0:T(128)} %pad_add_fusion.me_ref.place, bf16[2048,512]{1,0:T(8,128)(2,1)} %get-tuple-element.192.refs_0_.dq, bf16[2048,512]{1,0:T(8,128)(2,1)} %get-tuple-element.193.refs_1_.dk, bf16[2048,1024]{1,0:T(8,128)(2,1)} %get-tuple-element.194.refs_2_.dv, ...), custom_call_target="tpu_custom_call" | custom-call | flops 3959422976 | bytes 10485760 | tf_op jit(solution)/shard_map/pallas_call | solution.py:682
  206.7 2.1 collective-permute-done.11
  214.1 2.2 copy-done
  216.2 2.2 copy-done.4
  223.2 6.0 %shard_map.384.rest_0_ = bf16[2048,512]{1,0:T(8,128)(2,1)} custom-call(bf16[2048,512]{1,0:T(8,128)(2,1)S(1)} %copy-done.6, bf16[2048,512]{1,0:T(8,128)(2,1)S(1)} %copy-done.7, bf16[2048,1024]{1,0:T(8,128)(2,1)S(1)} %copy-done.4, bf16[2048,1024]{1,0:T(8,128)(2,1)S(1)} %copy-done, bf16[2048,512]{1,0:T(8,128)(2,1)S(1)} %bitcast.71, ...), custom_call_target="tpu_custom_call" | custom-call | flops 3221225472 | bytes 10485760 | tf_op jit(solution)/shard_map/pallas_call | solution.py:810
  229.3 2.5 collective-permute-start.16
  233.5 6.2 %shard_map.385 = bf16[2048,512]{1,0:T(8,128)(2,1)} custom-call(bf16[2048,512]{1,0:T(8,128)(2,1)S(1)} %copy-done.6, bf16[2048,512]{1,0:T(8,128)(2,1)S(1)} %copy-done.7, bf16[2048,1024]{1,0:T(8,128)(2,1)S(1)} %copy-done.4, bf16[2048,1024]{1,0:T(8,128)(2,1)S(1)} %copy-done, bf16[2048,512]{1,0:T(8,128)(2,1)S(1)} %bitcast.72, ...), custom_call_target="tpu_custom_call", output_to_operand_aliasing={{}: (9, {})} | custom-call | flops 3221225472 | bytes 10485760 | tf_op jit(solution)/shard_map/pallas_call | solution.py:810
  240.4 7.0 %collective-permute-done.17 = bf16[544,128]{1,0:T(8,128)(2,1)S(1)} collective-permute-done((bf16[544,128]{1,0:T(8,128)(2,1)S(1)}, bf16[544,128]{1,0:T(8,128)(2,1)S(1)}, u32[]{:S(2)}, u32[]{:S(2)}) %collective-permute-start.17) | collective-permute-done | bytes 139296 | tf_op jit(solution)/shard_map/ppermute | solution.py:72
  249.7 6.2 %collective-permute-done.18 = bf16[1088,128]{1,0:T(8,128)(2,1)S(1)} collective-permute-done((bf16[1088,128]{1,0:T(8,128)(2,1)S(1)}, bf16[1088,128]{1,0:T(8,128)(2,1)S(1)}, u32[]{:S(2)}, u32[]{:S(2)}) %collective-permute-start.18) | collective-permute-done | bytes 278560 | tf_op jit(solution)/shard_map/ppermute | solution.py:72
  255.9 2.6 collective-permute-done.20
  259.3 8.4 %collective-permute-done.21 = bf16[944,128]{1,0:T(8,128)(2,1)S(1)} collective-permute-done((bf16[944,128]{1,0:T(8,128)(2,1)S(1)}, bf16[944,128]{1,0:T(8,128)(2,1)S(1)}, u32[]{:S(2)}, u32[]{:S(2)}) %collective-permute-start.21) | collective-permute-done | bytes 241696 | tf_op jit(solution)/shard_map/ppermute | solution.py:72
  269.6 4.4 %collective-permute-done.22.refs_3_ = bf16[944,128]{1,0:T(8,128)(2,1)S(1)} collective-permute-done((bf16[944,128]{1,0:T(8,128)(2,1)S(1)}, bf16[944,128]{1,0:T(8,128)(2,1)S(1)}, u32[]{:S(2)}, u32[]{:S(2)}) %collective-permute-start.22) | collective-permute-done | bytes 241696 | tf_op jit(solution)/shard_map/ppermute | solution.py:72
  279.4 8.4 %shard_map.387 = (f32[2,128,512]{2,1,0:T(8,128)}, f32[2,864,128]{2,1,0:T(8,128)}, f32[864,128]{1,0:T(8,128)}, f32[2,864,128]{2,1,0:T(8,128)}, f32[864,128]{1,0:T...) custom-call(f32[8,128]{1,0:T(8,128)S(1)} %get-tuple-element.222.refs, ...), custom_call_target="tpu_custom_call" | custom-call | tf_op jit(solution)/shard_map/pallas_call | solution.py:936
  (159 shorter events, 49.9 us)
Async XLA Ops:
  7.2 60.0 %all-gather.2.cloned.1.call-start = ((), (), s32[]{:S(2)}) async-start(), calls=%async_computation | async-start | bytes 5939200 | tf_op jit(solution)/shard_map/all_gather | solution.py:997
  9.4 14.1 %collective-permute-start = (bf16[1904,128]{1,0:T(8,128)(2,1)S(1)}, bf16[1904,128]{1,0:T(8,128)(2,1)S(1)}, u32[]{:S(2)}, u32[]{:S(2)}) collective-permute-start(bf16[1904,128]{1,0:T(8,128)(2,1)S(1)} %fusion.5.refs_0_), channel_id=1, source_target_pairs={{0,2},{1,3},{2,0},{3,1},{4,6},{5,7},{6,4},{7,5},{8,10},{9,11},{10,... | collective-permute-start | bytes 1462280 | tf_op jit(solution)/shard_map/ppermute | solution.py:72
  23.6 5.6 %collective-permute-start.1 = (bf16[1904,128]{1,0:T(8,128)(2,1)S(1)}, bf16[1904,128]{1,0:T(8,128)(2,1)}, u32[]{:S(2)}, u32[]{:S(2)}) collective-permute-start(bf16[1904,128]{1,0:T(8,128)(2,1)S(1)} %fusion.5.refs_0_), channel_id=1, source_target_pairs={{0,1},{1,0},{2,3},{3,2},{4,5},{5,4},{6,7},{7,6},{8,9},{9,8},{10,11... | collective-permute-start | bytes 1462280 | tf_op jit(solution)/shard_map/ppermute | solution.py:72
  23.7 5.5 %collective-permute-start.2 = (bf16[1904,128]{1,0:T(8,128)(2,1)S(1)}, bf16[1904,128]{1,0:T(8,128)(2,1)}, u32[]{:S(2)}, u32[]{:S(2)}) collective-permute-start(bf16[1904,128]{1,0:T(8,128)(2,1)S(1)} %collective-permute-done.refs_1_), channel_id=1, source_target_pairs={{0,1},{1,0},{2,3},{3,2},{4,5},{5,4},{6,7},{7,6},{8,9},{9,8},{10,11... | collective-permute-start | bytes 1462280 | tf_op jit(solution)/shard_map/ppermute | solution.py:72
  43.5 4.5 %collective-permute-start.3 = (bf16[2,2,256,512]{3,2,1,0:T(8,128)(2,1)}, bf16[2,2,256,512]{3,2,1,0:T(8,128)(2,1)S(1)}, u32[]{:S(2)}, u32[]{:S(2)}) collective-permute-start(bf16[2,2,256,512]{3,2,1,0:T(8,128)(2,1)} %get-tuple-element.139.local), channel_id=1, source_target_pairs={{0,1},{2,3},{4,5},{6,7},{8,9},{10,11},{12,13},{14,15},{16,17},{18,... | collective-permute-start | bytes 3145736 | tf_op jit(solution)/shard_map/ppermute | solution.py:141
  52.7 11.7 %collective-permute-start.4 = (bf16[2,2,256,512]{3,2,1,0:T(8,128)(2,1)}, bf16[2,2,256,512]{3,2,1,0:T(8,128)(2,1)S(1)}, u32[]{:S(2)}, u32[]{:S(2)}) collective-permute-start(bf16[2,2,256,512]{3,2,1,0:T(8,128)(2,1)} %shard_map.375), channel_id=1, source_target_pairs={{1,2},{5,6},{9,10},{13,14},{17,18},{21,22},{25,26},{29,30}} | collective-permute-start | bytes 3145736 | tf_op jit(solution)/shard_map/ppermute | solution.py:146
  64.4 8.9 %collective-permute-start.5 = (bf16[2,2,256,512]{3,2,1,0:T(8,128)(2,1)S(1)}, bf16[2,2,256,512]{3,2,1,0:T(8,128)(2,1)}, u32[]{:S(2)}, u32[]{:S(2)}) collective-permute-start(bf16[2,2,256,512]{3,2,1,0:T(8,128)(2,1)S(1)} %collective-permute-done.4.refs_9_), channel_id=1, source_target_pairs={{2,3},{6,7},{10,11},{14,15},{18,19},{22,23},{26,27},{30,31}} | collective-permute-start | bytes 3145736 | tf_op jit(solution)/shard_map/ppermute | solution.py:150
  115.0 13.9 %collective-permute-start.6 = (bf16[2,2,256,512]{3,2,1,0:T(8,128)(2,1)}, bf16[2,2,256,512]{3,2,1,0:T(8,128)(2,1)S(1)}, u32[]{:S(2)}, u32[]{:S(2)}) collective-permute-start(bf16[2,2,256,512]{3,2,1,0:T(8,128)(2,1)} %get-tuple-element.162.local), channel_id=1, source_target_pairs={{3,2},{1,0},{7,6},{5,4},{11,10},{9,8},{15,14},{13,12},{19,18},{17,... | collective-permute-start | bytes 3145736 | tf_op jit(solution)/shard_map/ppermute | solution.py:141
  133.6 14.6 %collective-permute-start.7 = (bf16[2,2,256,512]{3,2,1,0:T(8,128)(2,1)}, bf16[2,2,256,512]{3,2,1,0:T(8,128)(2,1)S(1)}, u32[]{:S(2)}, u32[]{:S(2)}) collective-permute-start(bf16[2,2,256,512]{3,2,1,0:T(8,128)(2,1)} %shard_map.380), channel_id=1, source_target_pairs={{2,1},{6,5},{10,9},{14,13},{18,17},{22,21},{26,25},{30,29}} | collective-permute-start | bytes 3145736 | tf_op jit(solution)/shard_map/ppermute | solution.py:146
  148.2 12.7 %collective-permute-start.8 = (bf16[2,4352,128]{2,1,0:T(8,128)(2,1)}, bf16[2,4352,128]{2,1,0:T(8,128)(2,1)S(1)}, u32[]{:S(2)}, u32[]{:S(2)}) collective-permute-start(bf16[2,4352,128]{2,1,0:T(8,128)(2,1)} %get-tuple-element.185), channel_id=1, source_target_pairs={{0,1},{1,0},{2,3},{3,2},{4,5},{5,4},{6,7},{7,6},{8,9},{9,8},{10,11... | collective-permute-start | bytes 6684680 | tf_op jit(solution)/shard_map/ppermute | solution.py:72
  156.7 9.3 %collective-permute-start.9 = (bf16[2,2,256,512]{3,2,1,0:T(8,128)(2,1)S(1)}, bf16[2,2,256,512]{3,2,1,0:T(8,128)(2,1)S(1)}, u32[]{:S(2)}, u32[]{:S(2)}) collective-permute-start(bf16[2,2,256,512]{3,2,1,0:T(8,128)(2,1)S(1)} %collective-permute-done.7.refs_11_), channel_id=1, source_target_pairs={{1,0},{5,4},{9,8},{13,12},{17,16},{21,20},{25,24},{29,28}} | collective-permute-start | bytes 3145736 | tf_op jit(solution)/shard_map/ppermute | solution.py:150
  164.2 27.2 %collective-permute-start.10 = (bf16[4352,128]{1,0:T(8,128)(2,1)}, bf16[4352,128]{1,0:T(8,128)(2,1)}, u32[]{:S(2)}, u32[]{:S(2)}) collective-permute-start(bf16[4352,128]{1,0:T(8,128)(2,1)} %fusion), channel_id=1, source_target_pairs={{0,2},{1,3},{2,0},{3,1},{4,6},{5,7},{6,4},{7,5},{8,10},{9,11},{10,... | collective-permute-start | bytes 3342344 | tf_op jit(solution)/shard_map/ppermute | solution.py:72
  194.4 14.5 %collective-permute-start.11 = (bf16[2176,128]{1,0:T(8,128)(2,1)}, bf16[2176,128]{1,0:T(8,128)(2,1)}, u32[]{:S(2)}, u32[]{:S(2)}) collective-permute-start(bf16[2176,128]{1,0:T(8,128)(2,1)} %get-tuple-element.246), channel_id=1, source_target_pairs={{0,4},{4,0},{8,12},{12,8},{16,20},{20,16},{24,28},{28,24},{1,5},{5... | collective-permute-start | bytes 1671176 | tf_op jit(solution)/shard_map/ppermute | solution.py:72
  206.7 5.4 %collective-permute-start.12 = (bf16[2,1888,128]{2,1,0:T(8,128)(2,1)}, bf16[2,1888,128]{2,1,0:T(8,128)(2,1)S(1)}, u32[]{:S(2)}, u32[]{:S(2)}) collective-permute-start(bf16[2,1888,128]{2,1,0:T(8,128)(2,1)} %get-tuple-element.208), channel_id=1, source_target_pairs={{0,1},{1,0},{2,3},{3,2},{4,5},{5,4},{6,7},{7,6},{8,9},{9,8},{10,11... | collective-permute-start | bytes 2899976 | tf_op jit(solution)/shard_map/ppermute | solution.py:72
  210.4 18.9 %collective-permute-start.14 = (bf16[1088,128]{1,0:T(8,128)(2,1)S(1)}, bf16[1088,128]{1,0:T(8,128)(2,1)S(1)}, u32[]{:S(2)}, u32[]{:S(2)}) collective-permute-start(bf16[1088,128]{1,0:T(8,128)(2,1)S(1)} %get-tuple-element.248), channel_id=1, source_target_pairs={{0,8},{4,12},{8,0},{12,4},{16,24},{20,28},{24,16},{28,20},{1,9},{5... | collective-permute-start | bytes 835592 | tf_op jit(solution)/shard_map/ppermute | solution.py:72
  212.3 19.5 %collective-permute-start.13 = (bf16[1888,128]{1,0:T(8,128)(2,1)S(1)}, bf16[1888,128]{1,0:T(8,128)(2,1)S(1)}, u32[]{:S(2)}, u32[]{:S(2)}) collective-permute-start(bf16[1888,128]{1,0:T(8,128)(2,1)S(1)} %fusion.6), channel_id=1, source_target_pairs={{0,2},{1,3},{2,0},{3,1},{4,6},{5,7},{6,4},{7,5},{8,10},{9,11},{10,... | collective-permute-start | bytes 1449992 | tf_op jit(solution)/shard_map/ppermute | solution.py:72
  229.3 10.5 %collective-permute-start.16 = (bf16[544,128]{1,0:T(8,128)(2,1)S(1)}, bf16[544,128]{1,0:T(8,128)(2,1)S(1)}, u32[]{:S(2)}, u32[]{:S(2)}) collective-permute-start(bf16[544,128]{1,0:T(8,128)(2,1)S(1)} %add_convert_fusion.10), channel_id=1, source_target_pairs={{0,16},{4,20},{8,24},{12,28},{16,0},{20,4},{24,8},{28,12},{1,17},{... | collective-permute-start | bytes 417800 | tf_op jit(solution)/shard_map/ppermute | solution.py:72
  231.9 15.6 %collective-permute-start.15 = (bf16[1888,128]{1,0:T(8,128)(2,1)S(1)}, bf16[1888,128]{1,0:T(8,128)(2,1)S(1)}, u32[]{:S(2)}, u32[]{:S(2)}) collective-permute-start(bf16[1888,128]{1,0:T(8,128)(2,1)S(1)} %fusion.4), channel_id=1, source_target_pairs={{0,4},{4,0},{8,12},{12,8},{16,20},{20,16},{24,28},{28,24},{1,5},{5... | collective-permute-start | bytes 1449992 | tf_op jit(solution)/shard_map/ppermute | solution.py:72
  239.8 39.5 %copy-start.24 = (f32[864,128]{1,0:T(8,128)S(1)}, f32[864,128]{1,0:T(8,128)}, u32[]{:S(2)}) copy-start(f32[864,128]{1,0:T(8,128)} %refs_23_.1) | copy-start | bytes 1327108
  239.8 7.6 %collective-permute-start.17 = (bf16[544,128]{1,0:T(8,128)(2,1)S(1)}, bf16[544,128]{1,0:T(8,128)(2,1)S(1)}, u32[]{:S(2)}, u32[]{:S(2)}) collective-permute-start(bf16[544,128]{1,0:T(8,128)(2,1)S(1)} %add_convert_fusion.8), channel_id=1, source_target_pairs={{0,16},{4,20},{8,24},{12,28},{16,0},{20,4},{24,8},{28,12},{1,17},{... | collective-permute-start | bytes 417800 | tf_op jit(solution)/shard_map/ppermute | solution.py:72
  247.4 8.4 %collective-permute-start.18 = (bf16[1088,128]{1,0:T(8,128)(2,1)S(1)}, bf16[1088,128]{1,0:T(8,128)(2,1)S(1)}, u32[]{:S(2)}, u32[]{:S(2)}) collective-permute-start(bf16[1088,128]{1,0:T(8,128)(2,1)S(1)} %pad_maximum_fusion.1), channel_id=1, source_target_pairs={{0,8},{4,12},{8,0},{12,4},{16,24},{20,28},{24,16},{28,20},{1,9},{5... | collective-permute-start | bytes 835592 | tf_op jit(solution)/shard_map/ppermute | solution.py:72
  247.5 31.7 %copy-start.22 = (f32[864,128]{1,0:T(8,128)S(1)}, f32[864,128]{1,0:T(8,128)}, u32[]{:S(2)}) copy-start(f32[864,128]{1,0:T(8,128)} %refs_17_.1) | copy-start | bytes 1327108
  247.5 31.7 %copy-start.23 = (f32[864,128]{1,0:T(8,128)S(1)}, f32[864,128]{1,0:T(8,128)}, u32[]{:S(2)}) copy-start(f32[864,128]{1,0:T(8,128)} %refs_21_.1) | copy-start | bytes 1327108
  247.6 26.4 %copy-start.10 = (f32[2,128,512]{2,1,0:T(8,128)S(1)}, f32[2,128,512]{2,1,0:T(8,128)}, u32[]{:S(2)}) copy-start(f32[2,128,512]{2,1,0:T(8,128)} %refs_7_.3) | copy-start | bytes 1572868
  247.6 26.4 %copy-start.27 = (s32[3]{0:T(128)S(1)}, s32[3]{0:T(128)}, u32[]{:S(2)}) copy-start(s32[3]{0:T(128)} %pad_add_fusion.me_ref.place) | copy-start | bytes 40
  247.7 10.8 %collective-permute-start.20 = (bf16[944,128]{1,0:T(8,128)(2,1)S(1)}, bf16[944,128]{1,0:T(8,128)(2,1)S(1)}, u32[]{:S(2)}, u32[]{:S(2)}) collective-permute-start(bf16[944,128]{1,0:T(8,128)(2,1)S(1)} %add_convert_fusion.7), channel_id=1, source_target_pairs={{0,8},{4,12},{8,0},{12,4},{16,24},{20,28},{24,16},{28,20},{1,9},{5... | collective-permute-start | bytes 725000 | tf_op jit(solution)/shard_map/ppermute | solution.py:72
  258.6 9.2 %collective-permute-start.21 = (bf16[944,128]{1,0:T(8,128)(2,1)S(1)}, bf16[944,128]{1,0:T(8,128)(2,1)S(1)}, u32[]{:S(2)}, u32[]{:S(2)}) collective-permute-start(bf16[944,128]{1,0:T(8,128)(2,1)S(1)} %add_convert_fusion.5), channel_id=1, source_target_pairs={{0,16},{4,20},{8,24},{12,28},{16,0},{20,4},{24,8},{28,12},{1,17},{... | collective-permute-start | bytes 725000 | tf_op jit(solution)/shard_map/ppermute | solution.py:72
  258.7 10.9 %collective-permute-start.19 = (bf16[2176,128]{1,0:T(8,128)(2,1)S(1)}, bf16[2176,128]{1,0:T(8,128)(2,1)S(1)}, u32[]{:S(2)}, u32[]{:S(2)}) collective-permute-start(bf16[2176,128]{1,0:T(8,128)(2,1)S(1)} %pad_maximum_fusion.refs_0_), channel_id=1, source_target_pairs={{0,4},{4,0},{8,12},{12,8},{16,20},{20,16},{24,28},{28,24},{1,5},{5... | collective-permute-start | bytes 1671176 | tf_op jit(solution)/shard_map/ppermute | solution.py:72
  267.8 6.2 %collective-permute-start.22 = (bf16[944,128]{1,0:T(8,128)(2,1)S(1)}, bf16[944,128]{1,0:T(8,128)(2,1)S(1)}, u32[]{:S(2)}, u32[]{:S(2)}) collective-permute-start(bf16[944,128]{1,0:T(8,128)(2,1)S(1)} %add_convert_fusion.4.refs_2_), channel_id=1, source_target_pairs={{0,8},{4,12},{8,0},{12,4},{16,24},{20,28},{24,16},{28,20},{1,9},{5... | collective-permute-start | bytes 725000 | tf_op jit(solution)/shard_map/ppermute | solution.py:72
  275.6 3.0 %collective-permute-start.25 = (f32[8,128]{1,0:T(8,128)S(1)}, f32[8,128]{1,0:T(8,128)S(1)}, u32[]{:S(2)}, u32[]{:S(2)}) collective-permute-start(f32[8,128]{1,0:T(8,128)S(1)} %get-tuple-element.222.refs_0_), channel_id=1, source_target_pairs={{0,3},{1,2},{2,1},{3,0},{4,7},{5,6},{6,5},{7,4},{8,11},{9,10},{10,... | collective-permute-start | bytes 12296 | tf_op jit(solution)/shard_map/ppermute | solution.py:1087
  275.6 3.7 %collective-permute-start.24 = (f32[8,128]{1,0:T(8,128)S(1)}, f32[8,128]{1,0:T(8,128)S(1)}, u32[]{:S(2)}, u32[]{:S(2)}) collective-permute-start(f32[8,128]{1,0:T(8,128)S(1)} %get-tuple-element.222.refs_0_), channel_id=1, source_target_pairs={{0,2},{1,3},{2,0},{3,1},{4,6},{5,7},{6,4},{7,5},{8,10},{9,11},{10,... | collective-permute-start | bytes 12296 | tf_op jit(solution)/shard_map/ppermute | solution.py:1087
  276.0 3.3 %collective-permute-start.23 = (f32[8,128]{1,0:T(8,128)S(1)}, f32[8,128]{1,0:T(8,128)S(1)}, u32[]{:S(2)}, u32[]{:S(2)}) collective-permute-start(f32[8,128]{1,0:T(8,128)S(1)} %get-tuple-element.222.refs_0_), channel_id=1, source_target_pairs={{0,1},{1,0},{2,3},{3,2},{4,5},{5,4},{6,7},{7,6},{8,9},{9,8},{10,11... | collective-permute-start | bytes 12296 | tf_op jit(solution)/shard_map/ppermute | solution.py:1087
  (37 other events, 270.9 us)
Sparse Core Ops, SparseCore 0:
  23.7 39.7 all-gather.1
where the time goes:
time: 300 us; the launch traced here: 295 us
  Pallas kernels  155 us (52%)
  waiting for transfers between devices  51.7 us (17%)
  starting transfers between devices  37.1 us (12%)
  local copies, waits for them, and re-layouts  20.1 us (7%)
  other arithmetic  16 us (5%)
  between operations  15 us (5%)
    ppermute x17, waiting for transfers between devices, exchange(): return lax.ppermute(value, axis, [(i, i ^ 1 << bit) for i in range(size)])  47.4 us
    pallas_call x1, Pallas kernels, middle(): pl.pallas_call(functools.partial(middle_kernel, count, ff), grid=(seqs *...  41.8 us
    pallas_call x3, Pallas kernels, weight_grads(): pl.pallas_call(functools.partial(weight_kernel, plan, len(arrays), layout...  36.9 us
    ppermute x17, starting transfers between devices, exchange(): return lax.ppermute(value, axis, [(i, i ^ 1 << bit) for i in range(size)])  26.6 us
    unnamed x91, local copies, waits for them, and re-layouts  19.4 us
    pallas_call x1, Pallas kernels, back(): pl.pallas_call(functools.partial(back_kernel, count), grid=(seqs * count,...  18.1 us
    pallas_call x2, Pallas kernels, input_grad(): pl.pallas_call(input_kernel, grid=(steps,), out_shape=shape((rows, width)...  12.3 us
    pallas_call x1, Pallas kernels, front(): pl.pallas_call(functools.partial(front_kernel, count), grid=(seqs * count...  10.8 us
  transfers between devices with their start and end apart: 27, of which 13 were waited for; matrix products, arithmetic and copies ran while one was open for 6% of the time, Pallas kernels for 34%

commit v1 on v0

--- a/solution.py
+++ b/solution.py
@@ -72,10 +72,12 @@
     return lax.ppermute(value, axis, [(i, i ^ (1 << bit)) for i in range(size)])
 
 
-def gather_shards(own):
+def gather_shards(own, *others):
     held = [(0, own)]
     for bit in reversed(range(bits_of("shard"))):
-        held += [(mask | (1 << bit), exchange(part, "shard", bit)) for mask, part in held]
+        held += [
+            (mask | (1 << bit), after(exchange(part, "shard", bit), *others)) for mask, part in held
+        ]
     return [(mask, None, part) for mask, part in held]
 
 
@@ -687,7 +689,7 @@
         + [full(item.shape) for item in ready],
         out_specs=[full(item) for item in dims],
         scratch_shapes=[VMEM((height, width), WIDE)],
-        compiler_params=params(60),
+        compiler_params=params(48),
         cost_estimate=cost(2 * rows * used * width, 2 * rows * sum(i.shape[1] for i in arrays)),
     )(place, *arrays, *ready)
 
@@ -962,7 +964,7 @@
     me = lax.axis_index("shard").reshape(1)
     replica = lax.axis_index("dp")
     count = bits_of("dp")
-    halved = (tuple(range(count)), (1,))
+    halved = (tuple(range(count - 1)),) * 2
     numbers = [
         sum(((replica >> bit) & 1) << (len(bits) - 1 - i) for i, bit in enumerate(bits))
         for bits in halved
@@ -992,9 +994,6 @@
     rest = jnp.concatenate(
         [*heads(low(vg_t[1])), *heads(low(w_out)), low(gu_t[0]), low(gu_t[1]), low(w_down)]
     )
-    first_held = gather_shards(first)
-    rest = after(rest, first_held[1][2])
-    w_rest = lax.all_gather(rest, "shard", axis=1, tiled=True)
     side = (lax.axis_index("dp") & 1).reshape(1)
 
     half_width = KD // 2
@@ -1008,6 +1007,9 @@
     seg_col = segments.reshape(rows, 1)
     seg_row = segments.reshape(rows // BLOCK, 1, BLOCK)
     in_last = jnp.where(lax.axis_index("shard") > 0, segments[:, 0], -1)
+    first_held = gather_shards(first, cos, sin, seg_col, seg_row, in_last, place)
+    rest = after(rest, first_held[1][2])
+    w_rest = lax.all_gather(rest, "shard", axis=1, tiled=True)
     decay = log_decay
 
     def tick(*done):
@@ -1074,7 +1076,7 @@
     for part in range(2):
         grad_input = input_grad(part * blocks // 2, blocks // 2, *data, gains, grad_input)
         tick(grad_input)
-        tick(late.next(grad_input), early.next(grad_input))
+        tick((early, late)[part].next(grad_input))
     while early.left() or late.left():
         for item in (early, late):
             if item.left():

time: 300 us -> 297 us (0.990)
  Pallas kernels: 155 us -> 150 us
    pallas_call x3, Pallas kernels: 36.9 us -> 32.8 us  [weight_grads(): pl.pallas_call(functools.partial(weight_kernel, plan, len(arrays), layout...]
    unnamed x91 -> x106, local copies, waits for them, and re-layouts: 19.4 us -> 17.2 us
  transfers between devices with their start and end apart: 27 -> 27, of which waited for: 13 -> 16; matrix products, arithmetic and copies ran while one was open for 6% -> 6% of each run, Pallas kernels for 34% -> 32%
where the time goes in v1:
time: 297 us; the launch traced here: 291 us
  Pallas kernels  150 us (51%)
  waiting for transfers between devices  51.9 us (17%)
  starting transfers between devices  38.4 us (13%)
  local copies, waits for them, and re-layouts  19.3 us (6%)
  other arithmetic  16.8 us (6%)
  between operations  15.1 us (5%)
    ppermute x17, waiting for transfers between devices, exchange(): return lax.ppermute(value, axis, [(i, i ^ 1 << bit) for i in range(size)])  44.8 us
    pallas_call x1, Pallas kernels, middle(): pl.pallas_call(functools.partial(middle_kernel, count, ff), grid=(seqs *...  41.8 us
    pallas_call x3, Pallas kernels, weight_grads(): pl.pallas_call(functools.partial(weight_kernel, plan, len(arrays), layout...  32.8 us
    ppermute x17, starting transfers between devices, exchange(): return lax.ppermute(value, axis, [(i, i ^ 1 << bit) for i in range(size)])  28.7 us
    pallas_call x1, Pallas kernels, back(): pl.pallas_call(functools.partial(back_kernel, count), grid=(seqs * count,...  18.2 us
    unnamed x106, local copies, waits for them, and re-layouts  17.2 us
    pallas_call x2, Pallas kernels, input_grad(): pl.pallas_call(input_kernel, grid=(steps,), out_shape=shape((rows, width)...  12.4 us
    pallas_call x1, Pallas kernels, inner(): pl.pallas_call(inner_kernel, grid=(rows // BLOCK,), out_shape=[shape((row...  10.6 us
  transfers between devices with their start and end apart: 27, of which 16 were waited for; matrix products, arithmetic and copies ran while one was open for 6% of the time, Pallas kernels for 32%

profile of v1, /device:TPU:0, one launch (start us, length us, event | category | flops | bytes accessed | tf_op | source)
XLA Modules:
  0.0 291.3 jit_solution(4081059910363246008)
XLA Ops:
  9.4 3.0 %collective-permute-start = (bf16[1904,128]{1,0:T(8,128)(2,1)S(1)}, bf16[1904,128]{1,0:T(8,128)(2,1)S(1)}, u32[]{:S(2)}, u32[]{:S(2)}) collective-permute-start(bf16[1904,128]{1,0:T(8,128)(2,1)S(1)} %fusion.7.refs_0_), channel_id=1, source_target_pairs={{0,2},{1,3},{2,0},{3,1},{4,6},{5,7},{6,4},{7,5},{8,10},{9,11},{10,... | collective-permute-start | bytes 1462280 | tf_op jit(solution)/shard_map/ppermute | solution.py:72
  19.0 3.0 %multiply_sine_fusion = (f32[1024,128]{1,0:T(8,128)}, f32[1024,128]{1,0:T(8,128)}) fusion(f32[128]{0:T(128)S(1)} %multiply_exponential_fusion, f32[1024]{0:T(1024)S(1)} %add_convert_fusion.10), kind=kLoop, calls=%fused_computation.9 | loop fusion | flops 131072 | bytes 1053184 | tf_op jit(solution)/shard_map/sin | solution.py:1003
  28.5 10.4 %shard_map.374 = (bf16[2048,512]{1,0:T(8,128)(2,1)}, bf16[2048,512]{1,0:T(8,128)(2,1)}, bf16[2048,1024]{1,0:T(8,128)(2,1)}, f32[2,2,2,256,512]{4,3,2,1,0:T(8,128)}, bf16[2,2,256,512]{3,2,1,0:T(8,128)(2,1)}) custom-call(f32[2]{0:T(128)} %decay.5, s32[2,1024]{1,0:T(2,128)} %seg_s.5, bf16[2048,512]{1,0:T(8,128)(2,1)} %bitcast.72, bf16[2048,512]{1,0:T(8,128)(2,1)} %copy-done.1, ...), custom_call_target="tpu_custom_call" | custom-call | flops 4294967296 | bytes 12582912 | tf_op jit(solution)/shard_map/pallas_call | solution.py:289
  38.8 2.1 collective-permute-start.3
  40.9 2.4 collective-permute-done.3.got.refs_8_
  44.3 3.7 %shard_map.375 = bf16[2,2,256,512]{3,2,1,0:T(8,128)(2,1)} custom-call(f32[2]{0:T(128)} %decay.5, bf16[2,2,256,512]{3,2,1,0:T(8,128)(2,1)} %get-tuple-element.143.local, bf16[2,2,256,512]{3,2,1,0:T(8,128)(2,1)} %copy-done.43), custom_call_target="tpu_custom_call" | custom-call | flops 524288 | bytes 3145728 | tf_op jit(solution)/shard_map/pallas_call | solution.py:173
  48.8 10.6 %shard_map.376 = (bf16[2048,512]{1,0:T(8,128)(2,1)}, bf16[2048,1024]{1,0:T(8,128)(2,1)}) custom-call(f32[2]{0:T(128)} %decay.5, bf16[2048,512]{1,0:T(8,128)(2,1)} %get-tuple-element.151.k.refs_1_, bf16[2048,1024]{1,0:T(8,128)(2,1)} %get-tuple-element.152.v.refs_2_, bf16[2048,512]{1,0:T(8,128)(2,1)} %get-tuple-element.158.hid.refs_3_, ...), custom_call_target="tpu_custom_call" | custom-call | flops 3221225472 | bytes 16777216 | tf_op jit(solution)/shard_map/pallas_call | solution.py:338
  60.7 2.8 all-gather.2.cloned.1.call-done.w.refs_6_.w_gate
  63.5 6.1 %shard_map.377.refs_1_ = bf16[2048,1024]{1,0:T(8,128)(2,1)} custom-call(bf16[2048,512]{1,0:T(8,128)(2,1)} %get-tuple-element.158.hid.refs_3_, bf16[4640,512]{1,0:T(8,128)(2,1)} %all-gather.2.cloned.1.call-done.w.refs_6_.w_gate), custom_call_target="tpu_custom_call" | custom-call | flops 2147483648 | bytes 8388608 | tf_op jit(solution)/shard_map/pallas_call | solution.py:366
  70.6 41.8 %shard_map.378 = (bf16[2048,512]{1,0:T(8,128)(2,1)}, bf16[2048,512]{1,0:T(8,128)(2,1)}, bf16[2048,864]{1,0:T(8,128)(2,1)}, bf16[2048,864]{1,0:T(8,128)(2,1)}, bf...) custom-call(f32[2]{0:T(128)} %decay.5, ...), custom_call_target="tpu_custom_call" | custom-call | flops 15166603264 | bytes 31457280 | tf_op jit(solution)/shard_map/pallas_call | solution.py:602
  115.5 11.8 %shard_map.379.refs_4_ = bf16[2592,512]{1,0:T(8,128)(2,1)} custom-call(s32[3]{0:T(128)S(1)} %pad_add_fusion.me_ref.place, bf16[2048,864]{1,0:T(8,128)(2,1)} %get-tuple-element.170.refs_0_, bf16[2048,512]{1,0:T(8,128)(2,1)S(1)} %bitcast.85, bf16[2048,864]{1,0:T(8,128)(2,1)} %get-tuple-element.171.refs_2_, bf16[2048,512]{1,0:T(8,128)(2,1)S(1)} %copy-done.38, ...), custom_call_target="tpu_custom_call" | custom-call | flops 5435817984 | bytes 14811136 | tf_op jit(solution)/shard_map/pallas_call | solution.py:684
  128.3 3.8 %shard_map.380 = bf16[2,2,256,512]{3,2,1,0:T(8,128)(2,1)} custom-call(f32[2]{0:T(128)} %decay.5, bf16[2,2,256,512]{3,2,1,0:T(8,128)(2,1)} %get-tuple-element.166.local, bf16[2,2,256,512]{3,2,1,0:T(8,128)(2,1)} %copy-done.42), custom_call_target="tpu_custom_call" | custom-call | flops 524288 | bytes 3145728 | tf_op jit(solution)/shard_map/pallas_call | solution.py:173
  134.4 12.3 %shard_map.381 = (bf16[2,4352,128]{2,1,0:T(8,128)(2,1)}, bf16[2,4352,128]{2,1,0:T(8,128)(2,1)}) custom-call(s32[3]{0:T(128)S(1)} %pad_add_fusion.me_ref.place, bf16[2048,1024]{1,0:T(8,128)(2,1)} %get-tuple-element.181.refs_0_, bf16[2048,512]{1,0:T(8,128)(2,1)S(1)} %copy-done.4, bf16[2048,1024]{1,0:T(8,128)(2,1)} %get-tuple-element.183.refs_2_.ggate, ...), custom_call_target="tpu_custom_call" | custom-call | flops 3623878656 | bytes 12582912 | tf_op jit(solution)/shard_map/pallas_call | solution.py:684
  146.7 10.6 %collective-permute-start.8 = (bf16[2,4352,128]{2,1,0:T(8,128)(2,1)}, bf16[2,4352,128]{2,1,0:T(8,128)(2,1)S(1)}, u32[]{:S(2)}, u32[]{:S(2)}) collective-permute-start(bf16[2,4352,128]{2,1,0:T(8,128)(2,1)} %get-tuple-element.189), channel_id=1, source_target_pairs={{0,1},{1,0},{2,3},{3,2},{4,5},{5,4},{6,7},{7,6},{8,9},{9,8},{10,11... | collective-permute-start | bytes 6684680 | tf_op jit(solution)/shard_map/ppermute | solution.py:72
  158.8 2.7 collective-permute-done.8
  161.5 3.4 %fusion = bf16[4352,128]{1,0:T(8,128)(2,1)} fusion(bf16[2,4352,128]{2,1,0:T(8,128)(2,1)S(1)} %collective-permute-done.8, bf16[2,4352,128]{2,1,0:T(8,128)(2,1)} %get-tuple-element.184), kind=kLoop, calls=%fused_computation.1 | loop fusion | flops 2228224 | bytes 3342336 | tf_op jit(solution)/shard_map/convert_element_type | solution.py:85
  167.7 18.2 %shard_map.382 = (bf16[2048,512]{1,0:T(8,128)(2,1)}, bf16[2048,512]{1,0:T(8,128)(2,1)}, bf16[2048,1024]{1,0:T(8,128)(2,1)}) custom-call(f32[2]{0:T(128)} %decay.5, s32[2,1024]{1,0:T(2,128)} %seg_s.5, s32[2]{0:T(128)} %select_reduce_fusion.in_last, bf16[2048,512]{1,0:T(8,128)(2,1)} %get-tuple-element.154.refs_2_.refs_0_, ...), custom_call_target="tpu_custom_call" | custom-call | flops 9663676416 | bytes 33554432 | tf_op jit(solution)/shard_map/pallas_call | solution.py:770
  185.9 6.1 %collective-permute-done.10 = bf16[4352,128]{1,0:T(8,128)(2,1)S(1)} collective-permute-done((bf16[4352,128]{1,0:T(8,128)(2,1)}, bf16[4352,128]{1,0:T(8,128)(2,1)S(1)}, u32[]{:S(2)}, u32[]{:S(2)}) %collective-permute-start.10) | collective-permute-done | bytes 1114144 | tf_op jit(solution)/shard_map/ppermute | solution.py:72
  192.1 2.6 fusion.1
  196.4 8.7 %shard_map.383 = (bf16[2,1920,128]{2,1,0:T(8,128)(2,1)S(1)}, bf16[2,1920,128]{2,1,0:T(8,128)(2,1)S(1)}) custom-call(s32[3]{0:T(128)S(1)} %pad_add_fusion.me_ref.place, bf16[2048,512]{1,0:T(8,128)(2,1)S(1)} %copy-done.8, bf16[2048,512]{1,0:T(8,128)(2,1)S(1)} %copy-done.9, bf16[2048,1024]{1,0:T(8,128)(2,1)} %get-tuple-element.198.refs_2_.dv, ...), custom_call_target="tpu_custom_call" | custom-call | flops 3959422976 | bytes 10485760 | tf_op jit(solution)/shard_map/pallas_call | solution.py:684
  206.1 3.1 %collective-permute-done.11 = bf16[2176,128]{1,0:T(8,128)(2,1)} collective-permute-done((bf16[2176,128]{1,0:T(8,128)(2,1)}, bf16[2176,128]{1,0:T(8,128)(2,1)}, u32[]{:S(2)}, u32[]{:S(2)}) %collective-permute-start.11) | collective-permute-done | bytes 557088 | tf_op jit(solution)/shard_map/ppermute | solution.py:72
  218.2 6.1 %shard_map.384.rest_0_ = bf16[2048,512]{1,0:T(8,128)(2,1)} custom-call(bf16[2048,512]{1,0:T(8,128)(2,1)S(1)} %copy-done.8, bf16[2048,512]{1,0:T(8,128)(2,1)S(1)} %copy-done.10, bf16[2048,1024]{1,0:T(8,128)(2,1)S(1)} %copy-done.6, bf16[2048,1024]{1,0:T(8,128)(2,1)S(1)} %copy-done, bf16[2048,512]{1,0:T(8,128)(2,1)S(1)} %bitcast.74, ...), custom_call_target="tpu_custom_call" | custom-call | flops 3221225472 | bytes 10485760 | tf_op jit(solution)/shard_map/pallas_call | solution.py:812
  225.4 2.5 collective-permute-start.15
  227.9 6.3 %shard_map.385 = bf16[2048,512]{1,0:T(8,128)(2,1)} custom-call(bf16[2048,512]{1,0:T(8,128)(2,1)S(1)} %copy-done.8, bf16[2048,512]{1,0:T(8,128)(2,1)S(1)} %copy-done.10, bf16[2048,1024]{1,0:T(8,128)(2,1)S(1)} %copy-done.6, bf16[2048,1024]{1,0:T(8,128)(2,1)S(1)} %copy-done, bf16[2048,512]{1,0:T(8,128)(2,1)S(1)} %bitcast.75, ...), custom_call_target="tpu_custom_call", output_to_operand_aliasing={{}: (9, {})} | custom-call | flops 3221225472 | bytes 10485760 | tf_op jit(solution)/shard_map/pallas_call | solution.py:812
  234.2 4.5 %collective-permute-done.15 = bf16[1088,128]{1,0:T(8,128)(2,1)S(1)} collective-permute-done((bf16[1088,128]{1,0:T(8,128)(2,1)S(1)}, bf16[1088,128]{1,0:T(8,128)(2,1)S(1)}, u32[]{:S(2)}, u32[]{:S(2)}) %collective-permute-start.15) | collective-permute-done | bytes 278560 | tf_op jit(solution)/shard_map/ppermute | solution.py:72
  240.9 6.0 %collective-permute-done.18 = bf16[960,128]{1,0:T(8,128)(2,1)S(1)} collective-permute-done((bf16[960,128]{1,0:T(8,128)(2,1)S(1)}, bf16[960,128]{1,0:T(8,128)(2,1)S(1)}, u32[]{:S(2)}, u32[]{:S(2)}) %collective-permute-start.18) | collective-permute-done | bytes 245792 | tf_op jit(solution)/shard_map/ppermute | solution.py:72
  247.1 2.4 collective-permute-done.16
  249.5 2.5 collective-permute-done.19
  253.9 5.3 %collective-permute-done.20 = bf16[480,128]{1,0:T(8,128)(2,1)S(1)} collective-permute-done((bf16[480,128]{1,0:T(8,128)(2,1)S(1)}, bf16[480,128]{1,0:T(8,128)(2,1)S(1)}, u32[]{:S(2)}, u32[]{:S(2)}) %collective-permute-start.20) | collective-permute-done | bytes 122912 | tf_op jit(solution)/shard_map/ppermute | solution.py:72
  259.4 4.9 %collective-permute-done.21 = bf16[480,128]{1,0:T(8,128)(2,1)S(1)} collective-permute-done((bf16[480,128]{1,0:T(8,128)(2,1)S(1)}, bf16[480,128]{1,0:T(8,128)(2,1)S(1)}, u32[]{:S(2)}, u32[]{:S(2)}) %collective-permute-start.21) | collective-permute-done | bytes 122912 | tf_op jit(solution)/shard_map/ppermute | solution.py:72
  265.4 5.1 %collective-permute-done.22.refs_3_ = bf16[960,128]{1,0:T(8,128)(2,1)S(1)} collective-permute-done((bf16[960,128]{1,0:T(8,128)(2,1)S(1)}, bf16[960,128]{1,0:T(8,128)(2,1)S(1)}, u32[]{:S(2)}, u32[]{:S(2)}) %collective-permute-start.22) | collective-permute-done | bytes 245792 | tf_op jit(solution)/shard_map/ppermute | solution.py:72
  275.8 8.4 %shard_map.387 = (f32[2,128,512]{2,1,0:T(8,128)}, f32[2,864,128]{2,1,0:T(8,128)}, f32[864,128]{1,0:T(8,128)}, f32[2,864,128]{2,1,0:T(8,128)}, f32[864,128]{1,0:T...) custom-call(f32[8,128]{1,0:T(8,128)S(1)} %get-tuple-element.224.refs, ...), custom_call_target="tpu_custom_call" | custom-call | tf_op jit(solution)/shard_map/pallas_call | solution.py:938
  (175 shorter events, 53.0 us)
Async XLA Ops:
  7.2 56.3 %all-gather.2.cloned.1.call-start = ((), (), s32[]{:S(2)}) async-start(), calls=%async_computation | async-start | bytes 5939200 | tf_op jit(solution)/shard_map/all_gather | solution.py:1012
  9.4 14.1 %collective-permute-start = (bf16[1904,128]{1,0:T(8,128)(2,1)S(1)}, bf16[1904,128]{1,0:T(8,128)(2,1)S(1)}, u32[]{:S(2)}, u32[]{:S(2)}) collective-permute-start(bf16[1904,128]{1,0:T(8,128)(2,1)S(1)} %fusion.7.refs_0_), channel_id=1, source_target_pairs={{0,2},{1,3},{2,0},{3,1},{4,6},{5,7},{6,4},{7,5},{8,10},{9,11},{10,... | collective-permute-start | bytes 1462280 | tf_op jit(solution)/shard_map/ppermute | solution.py:72
  23.6 2.0 collective-permute-start.1
  23.7 2.5 collective-permute-start.2
  38.8 4.5 %collective-permute-start.3 = (bf16[2,2,256,512]{3,2,1,0:T(8,128)(2,1)}, bf16[2,2,256,512]{3,2,1,0:T(8,128)(2,1)S(1)}, u32[]{:S(2)}, u32[]{:S(2)}) collective-permute-start(bf16[2,2,256,512]{3,2,1,0:T(8,128)(2,1)} %get-tuple-element.143.local), channel_id=1, source_target_pairs={{0,1},{2,3},{4,5},{6,7},{8,9},{10,11},{12,13},{14,15},{16,17},{18,... | collective-permute-start | bytes 3145736 | tf_op jit(solution)/shard_map/ppermute | solution.py:143
  48.1 11.4 %collective-permute-start.4 = (bf16[2,2,256,512]{3,2,1,0:T(8,128)(2,1)}, bf16[2,2,256,512]{3,2,1,0:T(8,128)(2,1)S(1)}, u32[]{:S(2)}, u32[]{:S(2)}) collective-permute-start(bf16[2,2,256,512]{3,2,1,0:T(8,128)(2,1)} %shard_map.375), channel_id=1, source_target_pairs={{1,2},{5,6},{9,10},{13,14},{17,18},{21,22},{25,26},{29,30}} | collective-permute-start | bytes 3145736 | tf_op jit(solution)/shard_map/ppermute | solution.py:148
  59.4 10.2 %collective-permute-start.5 = (bf16[2,2,256,512]{3,2,1,0:T(8,128)(2,1)S(1)}, bf16[2,2,256,512]{3,2,1,0:T(8,128)(2,1)S(1)}, u32[]{:S(2)}, u32[]{:S(2)}) collective-permute-start(bf16[2,2,256,512]{3,2,1,0:T(8,128)(2,1)S(1)} %collective-permute-done.4.refs_9_), channel_id=1, source_target_pairs={{2,3},{6,7},{10,11},{14,15},{18,19},{22,23},{26,27},{30,31}} | collective-permute-start | bytes 3145736 | tf_op jit(solution)/shard_map/ppermute | solution.py:152
  70.6 43.3 %copy-start.37 = (bf16[2,1024,512]{2,1,0:T(8,128)(2,1)S(1)}, bf16[2,1024,512]{2,1,0:T(8,128)(2,1)}, u32[]{:S(2)}) copy-start(bf16[2,1024,512]{2,1,0:T(8,128)(2,1)} %param.23) | copy-start | bytes 6291460
  112.4 14.9 %collective-permute-start.6 = (bf16[2,2,256,512]{3,2,1,0:T(8,128)(2,1)}, bf16[2,2,256,512]{3,2,1,0:T(8,128)(2,1)S(1)}, u32[]{:S(2)}, u32[]{:S(2)}) collective-permute-start(bf16[2,2,256,512]{3,2,1,0:T(8,128)(2,1)} %get-tuple-element.166.local), channel_id=1, source_target_pairs={{3,2},{1,0},{7,6},{5,4},{11,10},{9,8},{15,14},{13,12},{19,18},{17,... | collective-permute-start | bytes 3145736 | tf_op jit(solution)/shard_map/ppermute | solution.py:143
  132.0 14.7 %collective-permute-start.7 = (bf16[2,2,256,512]{3,2,1,0:T(8,128)(2,1)}, bf16[2,2,256,512]{3,2,1,0:T(8,128)(2,1)S(1)}, u32[]{:S(2)}, u32[]{:S(2)}) collective-permute-start(bf16[2,2,256,512]{3,2,1,0:T(8,128)(2,1)} %shard_map.380), channel_id=1, source_target_pairs={{2,1},{6,5},{10,9},{14,13},{18,17},{22,21},{26,25},{30,29}} | collective-permute-start | bytes 3145736 | tf_op jit(solution)/shard_map/ppermute | solution.py:148
  146.7 14.8 %collective-permute-start.8 = (bf16[2,4352,128]{2,1,0:T(8,128)(2,1)}, bf16[2,4352,128]{2,1,0:T(8,128)(2,1)S(1)}, u32[]{:S(2)}, u32[]{:S(2)}) collective-permute-start(bf16[2,4352,128]{2,1,0:T(8,128)(2,1)} %get-tuple-element.189), channel_id=1, source_target_pairs={{0,1},{1,0},{2,3},{3,2},{4,5},{5,4},{6,7},{7,6},{8,9},{9,8},{10,11... | collective-permute-start | bytes 6684680 | tf_op jit(solution)/shard_map/ppermute | solution.py:72
  157.3 9.4 %collective-permute-start.9 = (bf16[2,2,256,512]{3,2,1,0:T(8,128)(2,1)S(1)}, bf16[2,2,256,512]{3,2,1,0:T(8,128)(2,1)S(1)}, u32[]{:S(2)}, u32[]{:S(2)}) collective-permute-start(bf16[2,2,256,512]{3,2,1,0:T(8,128)(2,1)S(1)} %collective-permute-done.7.refs_11_), channel_id=1, source_target_pairs={{1,0},{5,4},{9,8},{13,12},{17,16},{21,20},{25,24},{29,28}} | collective-permute-start | bytes 3145736 | tf_op jit(solution)/shard_map/ppermute | solution.py:152
  164.9 27.1 %collective-permute-start.10 = (bf16[4352,128]{1,0:T(8,128)(2,1)}, bf16[4352,128]{1,0:T(8,128)(2,1)S(1)}, u32[]{:S(2)}, u32[]{:S(2)}) collective-permute-start(bf16[4352,128]{1,0:T(8,128)(2,1)} %fusion), channel_id=1, source_target_pairs={{0,2},{1,3},{2,0},{3,1},{4,6},{5,7},{6,4},{7,5},{8,10},{9,11},{10,... | collective-permute-start | bytes 3342344 | tf_op jit(solution)/shard_map/ppermute | solution.py:72
  194.7 14.5 %collective-permute-start.11 = (bf16[2176,128]{1,0:T(8,128)(2,1)}, bf16[2176,128]{1,0:T(8,128)(2,1)}, u32[]{:S(2)}, u32[]{:S(2)}) collective-permute-start(bf16[2176,128]{1,0:T(8,128)(2,1)} %get-tuple-element.248), channel_id=1, source_target_pairs={{0,4},{4,0},{8,12},{12,8},{16,20},{20,16},{24,28},{28,24},{1,5},{5... | collective-permute-start | bytes 1671176 | tf_op jit(solution)/shard_map/ppermute | solution.py:72
  206.1 6.0 %collective-permute-start.12 = (bf16[2,1920,128]{2,1,0:T(8,128)(2,1)S(1)}, bf16[2,1920,128]{2,1,0:T(8,128)(2,1)S(1)}, u32[]{:S(2)}, u32[]{:S(2)}) collective-permute-start(bf16[2,1920,128]{2,1,0:T(8,128)(2,1)S(1)} %get-tuple-element.212), channel_id=1, source_target_pairs={{0,1},{1,0},{2,3},{3,2},{4,5},{5,4},{6,7},{7,6},{8,9},{9,8},{10,11... | collective-permute-start | bytes 2949128 | tf_op jit(solution)/shard_map/ppermute | solution.py:72
  210.3 14.0 %collective-permute-start.13 = (bf16[1088,128]{1,0:T(8,128)(2,1)S(1)}, bf16[1088,128]{1,0:T(8,128)(2,1)S(1)}, u32[]{:S(2)}, u32[]{:S(2)}) collective-permute-start(bf16[1088,128]{1,0:T(8,128)(2,1)S(1)} %add_convert_fusion.5), channel_id=1, source_target_pairs={{0,8},{4,12},{8,0},{12,4},{16,24},{20,28},{24,16},{28,20},{1,9},{5... | collective-permute-start | bytes 835592 | tf_op jit(solution)/shard_map/ppermute | solution.py:72
  213.3 25.5 %collective-permute-start.14 = (bf16[1920,128]{1,0:T(8,128)(2,1)S(1)}, bf16[1920,128]{1,0:T(8,128)(2,1)S(1)}, u32[]{:S(2)}, u32[]{:S(2)}) collective-permute-start(bf16[1920,128]{1,0:T(8,128)(2,1)S(1)} %fusion.4), channel_id=1, source_target_pairs={{0,2},{1,3},{2,0},{3,1},{4,6},{5,7},{6,4},{7,5},{8,10},{9,11},{10,... | collective-permute-start | bytes 1474568 | tf_op jit(solution)/shard_map/ppermute | solution.py:72
  225.4 13.3 %collective-permute-start.15 = (bf16[1088,128]{1,0:T(8,128)(2,1)S(1)}, bf16[1088,128]{1,0:T(8,128)(2,1)S(1)}, u32[]{:S(2)}, u32[]{:S(2)}) collective-permute-start(bf16[1088,128]{1,0:T(8,128)(2,1)S(1)} %add_convert_fusion.3), channel_id=1, source_target_pairs={{0,16},{4,20},{8,24},{12,28},{16,0},{20,4},{24,8},{28,12},{1,17},{... | collective-permute-start | bytes 835592 | tf_op jit(solution)/shard_map/ppermute | solution.py:72
  238.7 36.9 %copy-start.27 = (f32[2,128,512]{2,1,0:T(8,128)S(1)}, f32[2,128,512]{2,1,0:T(8,128)}, u32[]{:S(2)}) copy-start(f32[2,128,512]{2,1,0:T(8,128)} %refs_19_.1) | copy-start | bytes 1572868
  238.8 36.9 %copy-start.28 = (f32[864,128]{1,0:T(8,128)S(1)}, f32[864,128]{1,0:T(8,128)}, u32[]{:S(2)}) copy-start(f32[864,128]{1,0:T(8,128)} %refs_15_.1) | copy-start | bytes 1327108
  238.8 36.9 %copy-start.29 = (f32[864,128]{1,0:T(8,128)S(1)}, f32[864,128]{1,0:T(8,128)}, u32[]{:S(2)}) copy-start(f32[864,128]{1,0:T(8,128)} %refs_17_.1) | copy-start | bytes 1327108
  238.8 36.9 %copy-start.30 = (f32[864,128]{1,0:T(8,128)S(1)}, f32[864,128]{1,0:T(8,128)}, u32[]{:S(2)}) copy-start(f32[864,128]{1,0:T(8,128)} %refs_21_.1) | copy-start | bytes 1327108
  239.0 7.9 %collective-permute-start.18 = (bf16[960,128]{1,0:T(8,128)(2,1)S(1)}, bf16[960,128]{1,0:T(8,128)(2,1)S(1)}, u32[]{:S(2)}, u32[]{:S(2)}) collective-permute-start(bf16[960,128]{1,0:T(8,128)(2,1)S(1)} %get-tuple-element.250), channel_id=1, source_target_pairs={{0,4},{4,0},{8,12},{12,8},{16,20},{20,16},{24,28},{28,24},{1,5},{5... | collective-permute-start | bytes 737288 | tf_op jit(solution)/shard_map/ppermute | solution.py:72
  240.8 8.6 %collective-permute-start.16 = (bf16[1088,128]{1,0:T(8,128)(2,1)S(1)}, bf16[1088,128]{1,0:T(8,128)(2,1)S(1)}, u32[]{:S(2)}, u32[]{:S(2)}) collective-permute-start(bf16[1088,128]{1,0:T(8,128)(2,1)S(1)} %add_convert_fusion.2), channel_id=1, source_target_pairs={{0,8},{4,12},{8,0},{12,4},{16,24},{20,28},{24,16},{28,20},{1,9},{5... | collective-permute-start | bytes 835592 | tf_op jit(solution)/shard_map/ppermute | solution.py:72
  247.0 4.9 %collective-permute-start.19 = (bf16[480,128]{1,0:T(8,128)(2,1)S(1)}, bf16[480,128]{1,0:T(8,128)(2,1)S(1)}, u32[]{:S(2)}, u32[]{:S(2)}) collective-permute-start(bf16[480,128]{1,0:T(8,128)(2,1)S(1)} %add_convert_fusion.8), channel_id=1, source_target_pairs={{0,8},{4,12},{8,0},{12,4},{16,24},{20,28},{24,16},{28,20},{1,9},{5... | collective-permute-start | bytes 368648 | tf_op jit(solution)/shard_map/ppermute | solution.py:72
  252.0 7.2 %collective-permute-start.20 = (bf16[480,128]{1,0:T(8,128)(2,1)S(1)}, bf16[480,128]{1,0:T(8,128)(2,1)S(1)}, u32[]{:S(2)}, u32[]{:S(2)}) collective-permute-start(bf16[480,128]{1,0:T(8,128)(2,1)S(1)} %add_convert_fusion.7), channel_id=1, source_target_pairs={{0,16},{4,20},{8,24},{12,28},{16,0},{20,4},{24,8},{28,12},{1,17},{... | collective-permute-start | bytes 368648 | tf_op jit(solution)/shard_map/ppermute | solution.py:72
  252.3 13.1 %collective-permute-start.17 = (bf16[2176,128]{1,0:T(8,128)(2,1)S(1)}, bf16[2176,128]{1,0:T(8,128)(2,1)S(1)}, u32[]{:S(2)}, u32[]{:S(2)}) collective-permute-start(bf16[2176,128]{1,0:T(8,128)(2,1)S(1)} %pad_maximum_fusion.refs_0_), channel_id=1, source_target_pairs={{0,4},{4,0},{8,12},{12,8},{16,20},{20,16},{24,28},{28,24},{1,5},{5... | collective-permute-start | bytes 1671176 | tf_op jit(solution)/shard_map/ppermute | solution.py:72
  259.3 4.9 %collective-permute-start.21 = (bf16[480,128]{1,0:T(8,128)(2,1)S(1)}, bf16[480,128]{1,0:T(8,128)(2,1)S(1)}, u32[]{:S(2)}, u32[]{:S(2)}) collective-permute-start(bf16[480,128]{1,0:T(8,128)(2,1)S(1)} %add_convert_fusion.6), channel_id=1, source_target_pairs={{0,8},{4,12},{8,0},{12,4},{16,24},{20,28},{24,16},{28,20},{1,9},{5... | collective-permute-start | bytes 368648 | tf_op jit(solution)/shard_map/ppermute | solution.py:72
  264.2 6.3 %collective-permute-start.22 = (bf16[960,128]{1,0:T(8,128)(2,1)S(1)}, bf16[960,128]{1,0:T(8,128)(2,1)S(1)}, u32[]{:S(2)}, u32[]{:S(2)}) collective-permute-start(bf16[960,128]{1,0:T(8,128)(2,1)S(1)} %pad_maximum_fusion.1.refs_2_), channel_id=1, source_target_pairs={{0,4},{4,0},{8,12},{12,8},{16,20},{20,16},{24,28},{28,24},{1,5},{5... | collective-permute-start | bytes 737288 | tf_op jit(solution)/shard_map/ppermute | solution.py:72
  272.0 3.0 %collective-permute-start.25 = (f32[8,128]{1,0:T(8,128)S(1)}, f32[8,128]{1,0:T(8,128)S(1)}, u32[]{:S(2)}, u32[]{:S(2)}) collective-permute-start(f32[8,128]{1,0:T(8,128)S(1)} %get-tuple-element.224.refs_0_), channel_id=1, source_target_pairs={{0,3},{1,2},{2,1},{3,0},{4,7},{5,6},{6,5},{7,4},{8,11},{9,10},{10,... | collective-permute-start | bytes 12296 | tf_op jit(solution)/shard_map/ppermute | solution.py:1089
  272.0 3.7 %collective-permute-start.24 = (f32[8,128]{1,0:T(8,128)S(1)}, f32[8,128]{1,0:T(8,128)S(1)}, u32[]{:S(2)}, u32[]{:S(2)}) collective-permute-start(f32[8,128]{1,0:T(8,128)S(1)} %get-tuple-element.224.refs_0_), channel_id=1, source_target_pairs={{0,2},{1,3},{2,0},{3,1},{4,6},{5,7},{6,4},{7,5},{8,10},{9,11},{10,... | collective-permute-start | bytes 12296 | tf_op jit(solution)/shard_map/ppermute | solution.py:1089
  272.5 3.1 %collective-permute-start.23 = (f32[8,128]{1,0:T(8,128)S(1)}, f32[8,128]{1,0:T(8,128)S(1)}, u32[]{:S(2)}, u32[]{:S(2)}) collective-permute-start(f32[8,128]{1,0:T(8,128)S(1)} %get-tuple-element.224.refs_0_), channel_id=1, source_target_pairs={{0,1},{1,0},{2,3},{3,2},{4,5},{5,4},{6,7},{7,6},{8,9},{9,8},{10,11... | collective-permute-start | bytes 12296 | tf_op jit(solution)/shard_map/ppermute | solution.py:1089
  (45 other events, 429.5 us)
Sparse Core Ops, SparseCore 0:
  23.7 39.7 all-gather.1

commit v2 on v1

--- a/solution.py
+++ b/solution.py
@@ -796,7 +796,7 @@
     out[...] = (glow[...].astype(WIDE) + r * (gh - xhat * inner_product)).astype(LOW)
 
 
-def input_grad(first, steps, dq, dk, dv, ggate, tokens, glow, w, w_rest, gains, earlier):
+def input_grad(first, steps, dq, dk, dv, ggate, tokens, glow, w, w_rest, gains, earlier, hides):
     rows, width = tokens.shape
     parts = rows // BLOCK // steps
     arrays = [dq, dk, dv, ggate, tokens, glow]
@@ -817,7 +817,9 @@
         out_specs=block(tokens),
         input_output_aliases=aliases,
         compiler_params=params(32),
-        cost_estimate=cost(2 * rows * width * (w.shape[0] + H * VP) // parts, 20 * rows * width // parts),
+        cost_estimate=cost(2 * rows * width * (w.shape[0] + H * VP) // parts, 20 * rows * width // parts)
+        if hides
+        else cost(1, 1),
     )(*inputs)
 
 
@@ -1061,7 +1063,11 @@
         st, dst, returning.got,
     )
     tick(dq)
-    tick(early.next(dq))
+    blocks = rows // BLOCK
+    data = (dq, dk, dv, ggate, tok, glow, w_qkv, w_rest)
+    grad_input = input_grad(0, blocks // 2, *data, gains, None, False)
+    tick(grad_input)
+    tick(early.next(grad_input))
     plan = [(0, 3, [(0, 0, kd)]), (1, 3, [(0, kd, kd)]), (2, 3, halves(2 * kd))]
     made = weight_grads(
         [dq, dk, dv, hid], plan, place, shards, fit(2 * kd + vd, layouts[1]), layouts[1]
@@ -1070,13 +1076,9 @@
     tick(made[0])
     tick(early.next(made[0]))
     tick(late.cross(made[0]))
-    blocks = rows // BLOCK
-    data = (dq, dk, dv, ggate, tok, glow, w_qkv, w_rest)
-    grad_input = None
-    for part in range(2):
-        grad_input = input_grad(part * blocks // 2, blocks // 2, *data, gains, grad_input)
-        tick(grad_input)
-        tick((early, late)[part].next(grad_input))
+    grad_input = input_grad(blocks // 2, blocks // 2, *data, gains, grad_input, True)
+    tick(grad_input)
+    tick(late.next(grad_input), early.next(grad_input))
     while early.left() or late.left():
         for item in (early, late):
             if item.left():

time: 297 us -> 306 us (1.030)
  local copies, waits for them, and re-layouts: 19.3 us -> 26.1 us
    unnamed x106 -> x108, local copies, waits for them, and re-layouts: 17.2 us -> 24.1 us
where the time goes in v2:
time: 306 us; the launch traced here: 300 us
  Pallas kernels  151 us (49%)
  waiting for transfers between devices  51.3 us (17%)
  starting transfers between devices  39.8 us (13%)
  local copies, waits for them, and re-layouts  26.1 us (9%)
  other arithmetic  16.8 us (5%)
  between operations  15 us (5%)
    ppermute x17, waiting for transfers between devices, exchange(): return lax.ppermute(value, axis, [(i, i ^ 1 << bit) for i in range(size)])  46.4 us
    pallas_call x1, Pallas kernels, middle(): pl.pallas_call(functools.partial(middle_kernel, count, ff), grid=(seqs *...  41.9 us
    pallas_call x3, Pallas kernels, weight_grads(): pl.pallas_call(functools.partial(weight_kernel, plan, len(arrays), layout...  32.8 us
    ppermute x17, starting transfers between devices, exchange(): return lax.ppermute(value, axis, [(i, i ^ 1 << bit) for i in range(size)])  29.3 us
    unnamed x108, local copies, waits for them, and re-layouts  24.1 us
    pallas_call x1, Pallas kernels, back(): pl.pallas_call(functools.partial(back_kernel, count), grid=(seqs * count,...  18.2 us
    pallas_call x2, Pallas kernels, input_grad(): pl.pallas_call(input_kernel, grid=(steps,), out_shape=shape((rows, width)...  12.5 us
    pallas_call x1, Pallas kernels, front(): pl.pallas_call(functools.partial(front_kernel, count), grid=(seqs * count...  10.6 us
  transfers between devices with their start and end apart: 27, of which 16 were waited for; matrix products, arithmetic and copies ran while one was open for 6% of the time, Pallas kernels for 32%

profile of v2, /device:TPU:0, one launch (start us, length us, event | category | flops | bytes accessed | tf_op | source)
XLA Modules:
  0.0 300.4 jit_solution(1070387795709316005)
XLA Ops:
  9.4 3.0 collective-permute-start
  20.0 3.0 %multiply_sine_fusion = (f32[1024,128]{1,0:T(8,128)}, f32[1024,128]{1,0:T(8,128)}) fusion(f32[128]{0:T(128)S(1)} %multiply_exponential_fusion, f32[1024]{0:T(1024)S(1)} %add_convert_fusion.10), kind=kLoop, calls=%fused_computation.9 | loop fusion | flops 131072 | bytes 1053184 | tf_op jit(solution)/shard_map/sin | solution.py:1005
  29.8 10.6 %shard_map.374 = (bf16[2048,512]{1,0:T(8,128)(2,1)}, bf16[2048,512]{1,0:T(8,128)(2,1)}, bf16[2048,1024]{1,0:T(8,128)(2,1)}, f32[2,2,2,256,512]{4,3,2,1,0:T(8,128)}, bf16[2,2,256,512]{3,2,1,0:T(8,128)(2,1)}) custom-call(f32[2]{0:T(128)} %decay.5, s32[2,1024]{1,0:T(2,128)} %seg_s.5, bf16[2048,512]{1,0:T(8,128)(2,1)} %bitcast.72, bf16[2048,512]{1,0:T(8,128)(2,1)} %copy-done.2, ...), custom_call_target="tpu_custom_call" | custom-call | flops 4294967296 | bytes 12582912 | tf_op jit(solution)/shard_map/pallas_call | solution.py:289
  42.4 2.4 collective-permute-done.3.got.refs_8_
  45.8 3.7 %shard_map.375 = bf16[2,2,256,512]{3,2,1,0:T(8,128)(2,1)} custom-call(f32[2]{0:T(128)} %decay.5, bf16[2,2,256,512]{3,2,1,0:T(8,128)(2,1)} %get-tuple-element.141.local, bf16[2,2,256,512]{3,2,1,0:T(8,128)(2,1)} %copy-done.45), custom_call_target="tpu_custom_call" | custom-call | flops 524288 | bytes 3145728 | tf_op jit(solution)/shard_map/pallas_call | solution.py:173
  50.3 10.4 %shard_map.376 = (bf16[2048,512]{1,0:T(8,128)(2,1)}, bf16[2048,1024]{1,0:T(8,128)(2,1)}) custom-call(f32[2]{0:T(128)} %decay.5, bf16[2048,512]{1,0:T(8,128)(2,1)} %get-tuple-element.149.k.refs_1_, bf16[2048,1024]{1,0:T(8,128)(2,1)} %get-tuple-element.150.v.refs_2_, bf16[2048,512]{1,0:T(8,128)(2,1)} %get-tuple-element.156.hid.refs_3_, ...), custom_call_target="tpu_custom_call" | custom-call | flops 3221225472 | bytes 16777216 | tf_op jit(solution)/shard_map/pallas_call | solution.py:338
  60.7 2.2 collective-permute-start.5
  63.5 6.1 %shard_map.377.refs_1_ = bf16[2048,1024]{1,0:T(8,128)(2,1)} custom-call(bf16[2048,512]{1,0:T(8,128)(2,1)} %get-tuple-element.156.hid.refs_3_, bf16[4640,512]{1,0:T(8,128)(2,1)} %all-gather.2.cloned.1.call-done.w.refs_6_.w_gate), custom_call_target="tpu_custom_call" | custom-call | flops 2147483648 | bytes 8388608 | tf_op jit(solution)/shard_map/pallas_call | solution.py:366
  69.6 41.9 %shard_map.378 = (bf16[2048,512]{1,0:T(8,128)(2,1)}, bf16[2048,512]{1,0:T(8,128)(2,1)}, bf16[2048,864]{1,0:T(8,128)(2,1)}, bf16[2048,864]{1,0:T(8,128)(2,1)}, bf...) custom-call(f32[2]{0:T(128)} %decay.5, ...), custom_call_target="tpu_custom_call" | custom-call | flops 15166603264 | bytes 31457280 | tf_op jit(solution)/shard_map/pallas_call | solution.py:602
  114.5 11.8 %shard_map.379.refs_4_ = bf16[2592,512]{1,0:T(8,128)(2,1)} custom-call(s32[3]{0:T(128)S(1)} %pad_add_fusion.me_ref.place, bf16[2048,864]{1,0:T(8,128)(2,1)} %get-tuple-element.168.refs_0_, bf16[2048,512]{1,0:T(8,128)(2,1)S(1)} %bitcast.85, bf16[2048,864]{1,0:T(8,128)(2,1)} %get-tuple-element.169.refs_2_, bf16[2048,512]{1,0:T(8,128)(2,1)S(1)} %copy-done.39, ...), custom_call_target="tpu_custom_call" | custom-call | flops 5435817984 | bytes 14811136 | tf_op jit(solution)/shard_map/pallas_call | solution.py:684
  126.4 3.9 %shard_map.380 = bf16[2,2,256,512]{3,2,1,0:T(8,128)(2,1)} custom-call(f32[2]{0:T(128)} %decay.5, bf16[2,2,256,512]{3,2,1,0:T(8,128)(2,1)} %get-tuple-element.164.local, bf16[2,2,256,512]{3,2,1,0:T(8,128)(2,1)} %collective-permute-done.6.got.refs_10_), custom_call_target="tpu_custom_call" | custom-call | flops 524288 | bytes 3145728 | tf_op jit(solution)/shard_map/pallas_call | solution.py:173
  132.6 12.3 %shard_map.381 = (bf16[2,4352,128]{2,1,0:T(8,128)(2,1)}, bf16[2,4352,128]{2,1,0:T(8,128)(2,1)}) custom-call(s32[3]{0:T(128)S(1)} %pad_add_fusion.me_ref.place, bf16[2048,1024]{1,0:T(8,128)(2,1)} %get-tuple-element.179.refs_0_, bf16[2048,512]{1,0:T(8,128)(2,1)S(1)} %copy-done.5, bf16[2048,1024]{1,0:T(8,128)(2,1)} %get-tuple-element.181.refs_2_.ggate, ...), custom_call_target="tpu_custom_call" | custom-call | flops 3623878656 | bytes 12582912 | tf_op jit(solution)/shard_map/pallas_call | solution.py:684
  144.9 11.9 %collective-permute-start.8 = (bf16[2,4352,128]{2,1,0:T(8,128)(2,1)}, bf16[2,4352,128]{2,1,0:T(8,128)(2,1)S(1)}, u32[]{:S(2)}, u32[]{:S(2)}) collective-permute-start(bf16[2,4352,128]{2,1,0:T(8,128)(2,1)} %get-tuple-element.187), channel_id=1, source_target_pairs={{0,1},{1,0},{2,3},{3,2},{4,5},{5,4},{6,7},{7,6},{8,9},{9,8},{10,11... | collective-permute-start | bytes 6684680 | tf_op jit(solution)/shard_map/ppermute | solution.py:72
  158.3 2.7 collective-permute-done.8
  161.0 3.3 %fusion = bf16[4352,128]{1,0:T(8,128)(2,1)} fusion(bf16[2,4352,128]{2,1,0:T(8,128)(2,1)S(1)} %collective-permute-done.8, bf16[2,4352,128]{2,1,0:T(8,128)(2,1)} %get-tuple-element.182), kind=kLoop, calls=%fused_computation.1 | loop fusion | flops 2228224 | bytes 3342336 | tf_op jit(solution)/shard_map/convert_element_type | solution.py:85
  164.3 2.4 collective-permute-start.10
  167.7 18.2 %shard_map.382 = (bf16[2048,512]{1,0:T(8,128)(2,1)}, bf16[2048,512]{1,0:T(8,128)(2,1)}, bf16[2048,1024]{1,0:T(8,128)(2,1)}) custom-call(f32[2]{0:T(128)} %decay.5, s32[2,1024]{1,0:T(2,128)} %seg_s.5, s32[2]{0:T(128)} %select_reduce_fusion.in_last, bf16[2048,512]{1,0:T(8,128)(2,1)} %get-tuple-element.152.refs_2_.refs_0_, ...), custom_call_target="tpu_custom_call" | custom-call | flops 9663676416 | bytes 33554432 | tf_op jit(solution)/shard_map/pallas_call | solution.py:770
  189.7 2.2 copy-done.8
  196.7 6.2 %shard_map.383.rest_0_ = bf16[2048,512]{1,0:T(8,128)(2,1)} custom-call(bf16[2048,512]{1,0:T(8,128)(2,1)S(1)} %copy-done.12, bf16[2048,512]{1,0:T(8,128)(2,1)S(1)} %copy-done.14, bf16[2048,1024]{1,0:T(8,128)(2,1)S(1)} %copy-done.8, bf16[2048,1024]{1,0:T(8,128)(2,1)S(1)} %copy-done, bf16[2048,512]{1,0:T(8,128)(2,1)S(1)} %bitcast.74, ...), custom_call_target="tpu_custom_call" | custom-call | flops 1 | bytes 1 | tf_op jit(solution)/shard_map/pallas_call | solution.py:812
  202.9 2.8 fusion.1
  207.4 8.7 %shard_map.384 = (bf16[2,1920,128]{2,1,0:T(8,128)(2,1)S(1)}, bf16[2,1920,128]{2,1,0:T(8,128)(2,1)S(1)}) custom-call(s32[3]{0:T(128)S(1)} %pad_add_fusion.me_ref.place, bf16[2048,512]{1,0:T(8,128)(2,1)S(1)} %copy-done.13, bf16[2048,512]{1,0:T(8,128)(2,1)S(1)} %copy-done.15, bf16[2048,1024]{1,0:T(8,128)(2,1)} %get-tuple-element.196.dv.refs_2_, ...), custom_call_target="tpu_custom_call" | custom-call | flops 3959422976 | bytes 10485760 | tf_op jit(solution)/shard_map/pallas_call | solution.py:684
  216.2 4.4 %collective-permute-done.11 = bf16[2176,128]{1,0:T(8,128)(2,1)} collective-permute-done((bf16[2176,128]{1,0:T(8,128)(2,1)}, bf16[2176,128]{1,0:T(8,128)(2,1)}, u32[]{:S(2)}, u32[]{:S(2)}) %collective-permute-start.11) | collective-permute-done | bytes 557088 | tf_op jit(solution)/shard_map/ppermute | solution.py:72
  226.2 6.3 %shard_map.385 = bf16[2048,512]{1,0:T(8,128)(2,1)} custom-call(bf16[2048,512]{1,0:T(8,128)(2,1)S(1)} %copy-done.13, bf16[2048,512]{1,0:T(8,128)(2,1)S(1)} %copy-done.15, bf16[2048,1024]{1,0:T(8,128)(2,1)S(1)} %copy-done.9, bf16[2048,1024]{1,0:T(8,128)(2,1)S(1)} %copy-done.1, bf16[2048,512]{1,0:T(8,128)(2,1)S(1)} %bitcast.75, ...), custom_call_target="tpu_custom_call", output_to_operand_aliasing={{}: (9, {})} | custom-call | flops 3221225472 | bytes 10485760 | tf_op jit(solution)/shard_map/pallas_call | solution.py:812
  233.7 2.5 collective-permute-start.15
  236.1 11.8 %collective-permute-done.15 = bf16[1088,128]{1,0:T(8,128)(2,1)S(1)} collective-permute-done((bf16[1088,128]{1,0:T(8,128)(2,1)S(1)}, bf16[1088,128]{1,0:T(8,128)(2,1)S(1)}, u32[]{:S(2)}, u32[]{:S(2)}) %collective-permute-start.15) | collective-permute-done | bytes 278560 | tf_op jit(solution)/shard_map/ppermute | solution.py:72
  250.0 6.0 %collective-permute-done.18 = bf16[960,128]{1,0:T(8,128)(2,1)S(1)} collective-permute-done((bf16[960,128]{1,0:T(8,128)(2,1)S(1)}, bf16[960,128]{1,0:T(8,128)(2,1)S(1)}, u32[]{:S(2)}, u32[]{:S(2)}) %collective-permute-start.18) | collective-permute-done | bytes 245792 | tf_op jit(solution)/shard_map/ppermute | solution.py:72
  256.2 2.4 collective-permute-done.16
  258.6 2.4 collective-permute-done.19
  263.0 5.3 %collective-permute-done.20 = bf16[480,128]{1,0:T(8,128)(2,1)S(1)} collective-permute-done((bf16[480,128]{1,0:T(8,128)(2,1)S(1)}, bf16[480,128]{1,0:T(8,128)(2,1)S(1)}, u32[]{:S(2)}, u32[]{:S(2)}) %collective-permute-start.20) | collective-permute-done | bytes 122912 | tf_op jit(solution)/shard_map/ppermute | solution.py:72
  268.4 4.9 %collective-permute-done.21 = bf16[480,128]{1,0:T(8,128)(2,1)S(1)} collective-permute-done((bf16[480,128]{1,0:T(8,128)(2,1)S(1)}, bf16[480,128]{1,0:T(8,128)(2,1)S(1)}, u32[]{:S(2)}, u32[]{:S(2)}) %collective-permute-start.21) | collective-permute-done | bytes 122912 | tf_op jit(solution)/shard_map/ppermute | solution.py:72
  274.5 5.1 %collective-permute-done.22.refs_3_ = bf16[960,128]{1,0:T(8,128)(2,1)S(1)} collective-permute-done((bf16[960,128]{1,0:T(8,128)(2,1)S(1)}, bf16[960,128]{1,0:T(8,128)(2,1)S(1)}, u32[]{:S(2)}, u32[]{:S(2)}) %collective-permute-start.22) | collective-permute-done | bytes 245792 | tf_op jit(solution)/shard_map/ppermute | solution.py:72
  284.9 8.4 %shard_map.387 = (f32[2,128,512]{2,1,0:T(8,128)}, f32[2,864,128]{2,1,0:T(8,128)}, f32[864,128]{1,0:T(8,128)}, f32[2,864,128]{2,1,0:T(8,128)}, f32[864,128]{1,0:T...) custom-call(f32[8,128]{1,0:T(8,128)S(1)} %get-tuple-element.220.refs, ...), custom_call_target="tpu_custom_call" | custom-call | tf_op jit(solution)/shard_map/pallas_call | solution.py:940
  (177 shorter events, 56.1 us)
Async XLA Ops:
  7.2 56.3 %all-gather.2.cloned.1.call-start = ((), (), s32[]{:S(2)}) async-start(), calls=%async_computation | async-start | bytes 5939200 | tf_op jit(solution)/shard_map/all_gather | solution.py:1014
  9.4 14.1 %collective-permute-start = (bf16[1904,128]{1,0:T(8,128)(2,1)S(1)}, bf16[1904,128]{1,0:T(8,128)(2,1)S(1)}, u32[]{:S(2)}, u32[]{:S(2)}) collective-permute-start(bf16[1904,128]{1,0:T(8,128)(2,1)S(1)} %fusion.7.refs_0_), channel_id=1, source_target_pairs={{0,2},{1,3},{2,0},{3,1},{4,6},{5,7},{6,4},{7,5},{8,10},{9,11},{10,... | collective-permute-start | bytes 1462280 | tf_op jit(solution)/shard_map/ppermute | solution.py:72
  23.6 2.1 collective-permute-start.1
  23.7 2.7 collective-permute-start.2
  40.4 4.4 %collective-permute-start.3 = (bf16[2,2,256,512]{3,2,1,0:T(8,128)(2,1)}, bf16[2,2,256,512]{3,2,1,0:T(8,128)(2,1)S(1)}, u32[]{:S(2)}, u32[]{:S(2)}) collective-permute-start(bf16[2,2,256,512]{3,2,1,0:T(8,128)(2,1)} %get-tuple-element.141.local), channel_id=1, source_target_pairs={{0,1},{2,3},{4,5},{6,7},{8,9},{10,11},{12,13},{14,15},{16,17},{18,... | collective-permute-start | bytes 3145736 | tf_op jit(solution)/shard_map/ppermute | solution.py:143
  49.6 11.1 %collective-permute-start.4 = (bf16[2,2,256,512]{3,2,1,0:T(8,128)(2,1)}, bf16[2,2,256,512]{3,2,1,0:T(8,128)(2,1)S(1)}, u32[]{:S(2)}, u32[]{:S(2)}) collective-permute-start(bf16[2,2,256,512]{3,2,1,0:T(8,128)(2,1)} %shard_map.375), channel_id=1, source_target_pairs={{1,2},{5,6},{9,10},{13,14},{17,18},{21,22},{25,26},{29,30}} | collective-permute-start | bytes 3145736 | tf_op jit(solution)/shard_map/ppermute | solution.py:148
  60.7 8.9 %collective-permute-start.5 = (bf16[2,2,256,512]{3,2,1,0:T(8,128)(2,1)S(1)}, bf16[2,2,256,512]{3,2,1,0:T(8,128)(2,1)}, u32[]{:S(2)}, u32[]{:S(2)}) collective-permute-start(bf16[2,2,256,512]{3,2,1,0:T(8,128)(2,1)S(1)} %collective-permute-done.4.refs_9_), channel_id=1, source_target_pairs={{2,3},{6,7},{10,11},{14,15},{18,19},{22,23},{26,27},{30,31}} | collective-permute-start | bytes 3145736 | tf_op jit(solution)/shard_map/ppermute | solution.py:152
  69.6 43.4 %copy-start.38 = (bf16[2,1024,512]{2,1,0:T(8,128)(2,1)S(1)}, bf16[2,1024,512]{2,1,0:T(8,128)(2,1)}, u32[]{:S(2)}) copy-start(bf16[2,1024,512]{2,1,0:T(8,128)(2,1)} %param.23) | copy-start | bytes 6291460
  111.5 14.9 %collective-permute-start.6 = (bf16[2,2,256,512]{3,2,1,0:T(8,128)(2,1)}, bf16[2,2,256,512]{3,2,1,0:T(8,128)(2,1)}, u32[]{:S(2)}, u32[]{:S(2)}) collective-permute-start(bf16[2,2,256,512]{3,2,1,0:T(8,128)(2,1)} %get-tuple-element.164.local), channel_id=1, source_target_pairs={{3,2},{1,0},{7,6},{5,4},{11,10},{9,8},{15,14},{13,12},{19,18},{17,... | collective-permute-start | bytes 3145736 | tf_op jit(solution)/shard_map/ppermute | solution.py:143
  130.3 14.6 %collective-permute-start.7 = (bf16[2,2,256,512]{3,2,1,0:T(8,128)(2,1)}, bf16[2,2,256,512]{3,2,1,0:T(8,128)(2,1)S(1)}, u32[]{:S(2)}, u32[]{:S(2)}) collective-permute-start(bf16[2,2,256,512]{3,2,1,0:T(8,128)(2,1)} %shard_map.380), channel_id=1, source_target_pairs={{2,1},{6,5},{10,9},{14,13},{18,17},{22,21},{26,25},{30,29}} | collective-permute-start | bytes 3145736 | tf_op jit(solution)/shard_map/ppermute | solution.py:148
  144.9 16.1 %collective-permute-start.8 = (bf16[2,4352,128]{2,1,0:T(8,128)(2,1)}, bf16[2,4352,128]{2,1,0:T(8,128)(2,1)S(1)}, u32[]{:S(2)}, u32[]{:S(2)}) collective-permute-start(bf16[2,4352,128]{2,1,0:T(8,128)(2,1)} %get-tuple-element.187), channel_id=1, source_target_pairs={{0,1},{1,0},{2,3},{3,2},{4,5},{5,4},{6,7},{7,6},{8,9},{9,8},{10,11... | collective-permute-start | bytes 6684680 | tf_op jit(solution)/shard_map/ppermute | solution.py:72
  156.8 10.0 %collective-permute-start.9 = (bf16[2,2,256,512]{3,2,1,0:T(8,128)(2,1)S(1)}, bf16[2,2,256,512]{3,2,1,0:T(8,128)(2,1)S(1)}, u32[]{:S(2)}, u32[]{:S(2)}) collective-permute-start(bf16[2,2,256,512]{3,2,1,0:T(8,128)(2,1)S(1)} %collective-permute-done.7.refs_11_), channel_id=1, source_target_pairs={{1,0},{5,4},{9,8},{13,12},{17,16},{21,20},{25,24},{29,28}} | collective-permute-start | bytes 3145736 | tf_op jit(solution)/shard_map/ppermute | solution.py:152
  164.3 38.5 %collective-permute-start.10 = (bf16[4352,128]{1,0:T(8,128)(2,1)}, bf16[4352,128]{1,0:T(8,128)(2,1)}, u32[]{:S(2)}, u32[]{:S(2)}) collective-permute-start(bf16[4352,128]{1,0:T(8,128)(2,1)} %fusion), channel_id=1, source_target_pairs={{0,2},{1,3},{2,0},{3,1},{4,6},{5,7},{6,4},{7,5},{8,10},{9,11},{10,... | collective-permute-start | bytes 3342344 | tf_op jit(solution)/shard_map/ppermute | solution.py:72
  205.7 14.9 %collective-permute-start.11 = (bf16[2176,128]{1,0:T(8,128)(2,1)}, bf16[2176,128]{1,0:T(8,128)(2,1)}, u32[]{:S(2)}, u32[]{:S(2)}) collective-permute-start(bf16[2176,128]{1,0:T(8,128)(2,1)} %get-tuple-element.244), channel_id=1, source_target_pairs={{0,4},{4,0},{8,12},{12,8},{16,20},{20,16},{24,28},{28,24},{1,5},{5... | collective-permute-start | bytes 1671176 | tf_op jit(solution)/shard_map/ppermute | solution.py:72
  216.1 7.4 %collective-permute-start.12 = (bf16[2,1920,128]{2,1,0:T(8,128)(2,1)S(1)}, bf16[2,1920,128]{2,1,0:T(8,128)(2,1)S(1)}, u32[]{:S(2)}, u32[]{:S(2)}) collective-permute-start(bf16[2,1920,128]{2,1,0:T(8,128)(2,1)S(1)} %get-tuple-element.212), channel_id=1, source_target_pairs={{0,1},{1,0},{2,3},{3,2},{4,5},{5,4},{6,7},{7,6},{8,9},{9,8},{10,11... | collective-permute-start | bytes 2949128 | tf_op jit(solution)/shard_map/ppermute | solution.py:72
  221.7 10.8 %collective-permute-start.14 = (bf16[1088,128]{1,0:T(8,128)(2,1)S(1)}, bf16[1088,128]{1,0:T(8,128)(2,1)S(1)}, u32[]{:S(2)}, u32[]{:S(2)}) collective-permute-start(bf16[1088,128]{1,0:T(8,128)(2,1)S(1)} %add_convert_fusion.5), channel_id=1, source_target_pairs={{0,8},{4,12},{8,0},{12,4},{16,24},{20,28},{24,16},{28,20},{1,9},{5... | collective-permute-start | bytes 835592 | tf_op jit(solution)/shard_map/ppermute | solution.py:72
  223.7 24.2 %collective-permute-start.13 = (bf16[1920,128]{1,0:T(8,128)(2,1)S(1)}, bf16[1920,128]{1,0:T(8,128)(2,1)S(1)}, u32[]{:S(2)}, u32[]{:S(2)}) collective-permute-start(bf16[1920,128]{1,0:T(8,128)(2,1)S(1)} %fusion.4), channel_id=1, source_target_pairs={{0,2},{1,3},{2,0},{3,1},{4,6},{5,7},{6,4},{7,5},{8,10},{9,11},{10,... | collective-permute-start | bytes 1474568 | tf_op jit(solution)/shard_map/ppermute | solution.py:72
  233.7 14.2 %collective-permute-start.15 = (bf16[1088,128]{1,0:T(8,128)(2,1)S(1)}, bf16[1088,128]{1,0:T(8,128)(2,1)S(1)}, u32[]{:S(2)}, u32[]{:S(2)}) collective-permute-start(bf16[1088,128]{1,0:T(8,128)(2,1)S(1)} %add_convert_fusion.3), channel_id=1, source_target_pairs={{0,16},{4,20},{8,24},{12,28},{16,0},{20,4},{24,8},{28,12},{1,17},{... | collective-permute-start | bytes 835592 | tf_op jit(solution)/shard_map/ppermute | solution.py:72
  247.9 36.9 %copy-start.32 = (f32[864,128]{1,0:T(8,128)S(1)}, f32[864,128]{1,0:T(8,128)}, u32[]{:S(2)}) copy-start(f32[864,128]{1,0:T(8,128)} %refs_23_.1) | copy-start | bytes 1327108
  248.1 7.9 %collective-permute-start.18 = (bf16[960,128]{1,0:T(8,128)(2,1)S(1)}, bf16[960,128]{1,0:T(8,128)(2,1)S(1)}, u32[]{:S(2)}, u32[]{:S(2)}) collective-permute-start(bf16[960,128]{1,0:T(8,128)(2,1)S(1)} %get-tuple-element.246), channel_id=1, source_target_pairs={{0,4},{4,0},{8,12},{12,8},{16,20},{20,16},{24,28},{28,24},{1,5},{5... | collective-permute-start | bytes 737288 | tf_op jit(solution)/shard_map/ppermute | solution.py:72
  249.9 34.9 %copy-start.29 = (f32[864,128]{1,0:T(8,128)S(1)}, f32[864,128]{1,0:T(8,128)}, u32[]{:S(2)}) copy-start(f32[864,128]{1,0:T(8,128)} %refs_15_.1) | copy-start | bytes 1327108
  249.9 34.9 %copy-start.30 = (f32[864,128]{1,0:T(8,128)S(1)}, f32[864,128]{1,0:T(8,128)}, u32[]{:S(2)}) copy-start(f32[864,128]{1,0:T(8,128)} %refs_17_.1) | copy-start | bytes 1327108
  249.9 34.9 %copy-start.31 = (f32[864,128]{1,0:T(8,128)S(1)}, f32[864,128]{1,0:T(8,128)}, u32[]{:S(2)}) copy-start(f32[864,128]{1,0:T(8,128)} %refs_21_.1) | copy-start | bytes 1327108
  249.9 8.7 %collective-permute-start.16 = (bf16[1088,128]{1,0:T(8,128)(2,1)S(1)}, bf16[1088,128]{1,0:T(8,128)(2,1)S(1)}, u32[]{:S(2)}, u32[]{:S(2)}) collective-permute-start(bf16[1088,128]{1,0:T(8,128)(2,1)S(1)} %add_convert_fusion.2), channel_id=1, source_target_pairs={{0,8},{4,12},{8,0},{12,4},{16,24},{20,28},{24,16},{28,20},{1,9},{5... | collective-permute-start | bytes 835592 | tf_op jit(solution)/shard_map/ppermute | solution.py:72
  256.1 4.9 %collective-permute-start.19 = (bf16[480,128]{1,0:T(8,128)(2,1)S(1)}, bf16[480,128]{1,0:T(8,128)(2,1)S(1)}, u32[]{:S(2)}, u32[]{:S(2)}) collective-permute-start(bf16[480,128]{1,0:T(8,128)(2,1)S(1)} %add_convert_fusion.8), channel_id=1, source_target_pairs={{0,8},{4,12},{8,0},{12,4},{16,24},{20,28},{24,16},{28,20},{1,9},{5... | collective-permute-start | bytes 368648 | tf_op jit(solution)/shard_map/ppermute | solution.py:72
  261.1 7.2 %collective-permute-start.20 = (bf16[480,128]{1,0:T(8,128)(2,1)S(1)}, bf16[480,128]{1,0:T(8,128)(2,1)S(1)}, u32[]{:S(2)}, u32[]{:S(2)}) collective-permute-start(bf16[480,128]{1,0:T(8,128)(2,1)S(1)} %add_convert_fusion.7), channel_id=1, source_target_pairs={{0,16},{4,20},{8,24},{12,28},{16,0},{20,4},{24,8},{28,12},{1,17},{... | collective-permute-start | bytes 368648 | tf_op jit(solution)/shard_map/ppermute | solution.py:72
  261.4 13.1 %collective-permute-start.17 = (bf16[2176,128]{1,0:T(8,128)(2,1)S(1)}, bf16[2176,128]{1,0:T(8,128)(2,1)S(1)}, u32[]{:S(2)}, u32[]{:S(2)}) collective-permute-start(bf16[2176,128]{1,0:T(8,128)(2,1)S(1)} %pad_maximum_fusion.refs_0_), channel_id=1, source_target_pairs={{0,4},{4,0},{8,12},{12,8},{16,20},{20,16},{24,28},{28,24},{1,5},{5... | collective-permute-start | bytes 1671176 | tf_op jit(solution)/shard_map/ppermute | solution.py:72
  268.4 4.9 %collective-permute-start.21 = (bf16[480,128]{1,0:T(8,128)(2,1)S(1)}, bf16[480,128]{1,0:T(8,128)(2,1)S(1)}, u32[]{:S(2)}, u32[]{:S(2)}) collective-permute-start(bf16[480,128]{1,0:T(8,128)(2,1)S(1)} %add_convert_fusion.6), channel_id=1, source_target_pairs={{0,8},{4,12},{8,0},{12,4},{16,24},{20,28},{24,16},{28,20},{1,9},{5... | collective-permute-start | bytes 368648 | tf_op jit(solution)/shard_map/ppermute | solution.py:72
  273.3 6.3 %collective-permute-start.22 = (bf16[960,128]{1,0:T(8,128)(2,1)S(1)}, bf16[960,128]{1,0:T(8,128)(2,1)S(1)}, u32[]{:S(2)}, u32[]{:S(2)}) collective-permute-start(bf16[960,128]{1,0:T(8,128)(2,1)S(1)} %pad_maximum_fusion.1.refs_2_), channel_id=1, source_target_pairs={{0,4},{4,0},{8,12},{12,8},{16,20},{20,16},{24,28},{28,24},{1,5},{5... | collective-permute-start | bytes 737288 | tf_op jit(solution)/shard_map/ppermute | solution.py:72
  281.1 3.0 %collective-permute-start.25 = (f32[8,128]{1,0:T(8,128)S(1)}, f32[8,128]{1,0:T(8,128)S(1)}, u32[]{:S(2)}, u32[]{:S(2)}) collective-permute-start(f32[8,128]{1,0:T(8,128)S(1)} %get-tuple-element.220.refs_0_), channel_id=1, source_target_pairs={{0,3},{1,2},{2,1},{3,0},{4,7},{5,6},{6,5},{7,4},{8,11},{9,10},{10,... | collective-permute-start | bytes 12296 | tf_op jit(solution)/shard_map/ppermute | solution.py:1091
  281.1 3.7 %collective-permute-start.24 = (f32[8,128]{1,0:T(8,128)S(1)}, f32[8,128]{1,0:T(8,128)S(1)}, u32[]{:S(2)}, u32[]{:S(2)}) collective-permute-start(f32[8,128]{1,0:T(8,128)S(1)} %get-tuple-element.220.refs_0_), channel_id=1, source_target_pairs={{0,2},{1,3},{2,0},{3,1},{4,6},{5,7},{6,4},{7,5},{8,10},{9,11},{10,... | collective-permute-start | bytes 12296 | tf_op jit(solution)/shard_map/ppermute | solution.py:1091
  282.6 2.2 collective-permute-start.23
  (46 other events, 327.7 us)
Sparse Core Ops, SparseCore 0:
  23.7 39.7 all-gather.1

commit v3 on v1

--- a/solution.py
+++ b/solution.py
@@ -1076,7 +1076,9 @@
     for part in range(2):
         grad_input = input_grad(part * blocks // 2, blocks // 2, *data, gains, grad_input)
         tick(grad_input)
-        tick((early, late)[part].next(grad_input))
+        sent = (early, late)[part].next(grad_input)
+        tick(sent)
+    early.next(sent)
     while early.left() or late.left():
         for item in (early, late):
             if item.left():

time: 297 us -> 297 us (level)
  no operation moved by 1% of the time
where the time goes in v3:
time: 297 us; the launch traced here: 291 us
  Pallas kernels  150 us (51%)
  waiting for transfers between devices  50.6 us (17%)
  starting transfers between devices  39.5 us (13%)
  local copies, waits for them, and re-layouts  19.3 us (6%)
  other arithmetic  16.8 us (6%)
  between operations  15.1 us (5%)
    ppermute x17, waiting for transfers between devices, exchange(): return lax.ppermute(value, axis, [(i, i ^ 1 << bit) for i in range(size)])  43.6 us
    pallas_call x1, Pallas kernels, middle(): pl.pallas_call(functools.partial(middle_kernel, count, ff), grid=(seqs *...  41.8 us
    pallas_call x3, Pallas kernels, weight_grads(): pl.pallas_call(functools.partial(weight_kernel, plan, len(arrays), layout...  32.8 us
    ppermute x17, starting transfers between devices, exchange(): return lax.ppermute(value, axis, [(i, i ^ 1 << bit) for i in range(size)])  29.8 us
    pallas_call x1, Pallas kernels, back(): pl.pallas_call(functools.partial(back_kernel, count), grid=(seqs * count,...  18.2 us
    unnamed x106, local copies, waits for them, and re-layouts  17.3 us
    pallas_call x2, Pallas kernels, input_grad(): pl.pallas_call(input_kernel, grid=(steps,), out_shape=shape((rows, width)...  12.4 us
    pallas_call x1, Pallas kernels, inner(): pl.pallas_call(inner_kernel, grid=(rows // BLOCK,), out_shape=[shape((row...  10.6 us
  transfers between devices with their start and end apart: 27, of which 16 were waited for; matrix products, arithmetic and copies ran while one was open for 6% of the time, Pallas kernels for 32%

profile of v3, /device:TPU:0, one launch (start us, length us, event | category | flops | bytes accessed | tf_op | source)
XLA Modules:
  0.0 291.2 jit_solution(17841947549245310246)
XLA Ops:
  9.4 3.0 %collective-permute-start = (bf16[1904,128]{1,0:T(8,128)(2,1)S(1)}, bf16[1904,128]{1,0:T(8,128)(2,1)S(1)}, u32[]{:S(2)}, u32[]{:S(2)}) collective-permute-start(bf16[1904,128]{1,0:T(8,128)(2,1)S(1)} %fusion.7.refs_0_), channel_id=1, source_target_pairs={{0,2},{1,3},{2,0},{3,1},{4,6},{5,7},{6,4},{7,5},{8,10},{9,11},{10,... | collective-permute-start | bytes 1462280 | tf_op jit(solution)/shard_map/ppermute | solution.py:72
  19.0 3.0 %multiply_sine_fusion = (f32[1024,128]{1,0:T(8,128)}, f32[1024,128]{1,0:T(8,128)}) fusion(f32[128]{0:T(128)S(1)} %multiply_exponential_fusion, f32[1024]{0:T(1024)S(1)} %add_convert_fusion.10), kind=kLoop, calls=%fused_computation.9 | loop fusion | flops 131072 | bytes 1053184 | tf_op jit(solution)/shard_map/sin | solution.py:1003
  28.5 10.4 %shard_map.374 = (bf16[2048,512]{1,0:T(8,128)(2,1)}, bf16[2048,512]{1,0:T(8,128)(2,1)}, bf16[2048,1024]{1,0:T(8,128)(2,1)}, f32[2,2,2,256,512]{4,3,2,1,0:T(8,128)}, bf16[2,2,256,512]{3,2,1,0:T(8,128)(2,1)}) custom-call(f32[2]{0:T(128)} %decay.5, s32[2,1024]{1,0:T(2,128)} %seg_s.5, bf16[2048,512]{1,0:T(8,128)(2,1)} %bitcast.72, bf16[2048,512]{1,0:T(8,128)(2,1)} %copy-done.1, ...), custom_call_target="tpu_custom_call" | custom-call | flops 4294967296 | bytes 12582912 | tf_op jit(solution)/shard_map/pallas_call | solution.py:289
  38.8 2.1 collective-permute-start.3
  40.9 2.4 collective-permute-done.3.got.refs_8_
  44.3 3.7 %shard_map.375 = bf16[2,2,256,512]{3,2,1,0:T(8,128)(2,1)} custom-call(f32[2]{0:T(128)} %decay.5, bf16[2,2,256,512]{3,2,1,0:T(8,128)(2,1)} %get-tuple-element.144.local, bf16[2,2,256,512]{3,2,1,0:T(8,128)(2,1)} %copy-done.43), custom_call_target="tpu_custom_call" | custom-call | flops 524288 | bytes 3145728 | tf_op jit(solution)/shard_map/pallas_call | solution.py:173
  48.8 10.6 %shard_map.376 = (bf16[2048,512]{1,0:T(8,128)(2,1)}, bf16[2048,1024]{1,0:T(8,128)(2,1)}) custom-call(f32[2]{0:T(128)} %decay.5, bf16[2048,512]{1,0:T(8,128)(2,1)} %get-tuple-element.152.k.refs_1_, bf16[2048,1024]{1,0:T(8,128)(2,1)} %get-tuple-element.153.v.refs_2_, bf16[2048,512]{1,0:T(8,128)(2,1)} %get-tuple-element.159.hid.refs_3_, ...), custom_call_target="tpu_custom_call" | custom-call | flops 3221225472 | bytes 16777216 | tf_op jit(solution)/shard_map/pallas_call | solution.py:338
  60.7 2.8 all-gather.2.cloned.1.call-done.w.refs_6_.w_gate
  63.5 6.1 %shard_map.377.refs_1_ = bf16[2048,1024]{1,0:T(8,128)(2,1)} custom-call(bf16[2048,512]{1,0:T(8,128)(2,1)} %get-tuple-element.159.hid.refs_3_, bf16[4640,512]{1,0:T(8,128)(2,1)} %all-gather.2.cloned.1.call-done.w.refs_6_.w_gate), custom_call_target="tpu_custom_call" | custom-call | flops 2147483648 | bytes 8388608 | tf_op jit(solution)/shard_map/pallas_call | solution.py:366
  70.6 41.8 %shard_map.378 = (bf16[2048,512]{1,0:T(8,128)(2,1)}, bf16[2048,512]{1,0:T(8,128)(2,1)}, bf16[2048,864]{1,0:T(8,128)(2,1)}, bf16[2048,864]{1,0:T(8,128)(2,1)}, bf...) custom-call(f32[2]{0:T(128)} %decay.5, ...), custom_call_target="tpu_custom_call" | custom-call | flops 15166603264 | bytes 31457280 | tf_op jit(solution)/shard_map/pallas_call | solution.py:602
  115.5 11.8 %shard_map.379.refs_4_ = bf16[2592,512]{1,0:T(8,128)(2,1)} custom-call(s32[3]{0:T(128)S(1)} %pad_add_fusion.me_ref.place, bf16[2048,864]{1,0:T(8,128)(2,1)} %get-tuple-element.171.refs_0_, bf16[2048,512]{1,0:T(8,128)(2,1)S(1)} %bitcast.85, bf16[2048,864]{1,0:T(8,128)(2,1)} %get-tuple-element.172.refs_2_, bf16[2048,512]{1,0:T(8,128)(2,1)S(1)} %copy-done.38, ...), custom_call_target="tpu_custom_call" | custom-call | flops 5435817984 | bytes 14811136 | tf_op jit(solution)/shard_map/pallas_call | solution.py:684
  128.3 3.8 %shard_map.380 = bf16[2,2,256,512]{3,2,1,0:T(8,128)(2,1)} custom-call(f32[2]{0:T(128)} %decay.5, bf16[2,2,256,512]{3,2,1,0:T(8,128)(2,1)} %get-tuple-element.167.local, bf16[2,2,256,512]{3,2,1,0:T(8,128)(2,1)} %copy-done.42), custom_call_target="tpu_custom_call" | custom-call | flops 524288 | bytes 3145728 | tf_op jit(solution)/shard_map/pallas_call | solution.py:173
  134.4 12.3 %shard_map.381 = (bf16[2,4352,128]{2,1,0:T(8,128)(2,1)}, bf16[2,4352,128]{2,1,0:T(8,128)(2,1)}) custom-call(s32[3]{0:T(128)S(1)} %pad_add_fusion.me_ref.place, bf16[2048,1024]{1,0:T(8,128)(2,1)} %get-tuple-element.182.refs_0_, bf16[2048,512]{1,0:T(8,128)(2,1)S(1)} %copy-done.4, bf16[2048,1024]{1,0:T(8,128)(2,1)} %get-tuple-element.184.refs_2_.ggate, ...), custom_call_target="tpu_custom_call" | custom-call | flops 3623878656 | bytes 12582912 | tf_op jit(solution)/shard_map/pallas_call | solution.py:684
  146.7 10.6 %collective-permute-start.8 = (bf16[2,4352,128]{2,1,0:T(8,128)(2,1)}, bf16[2,4352,128]{2,1,0:T(8,128)(2,1)S(1)}, u32[]{:S(2)}, u32[]{:S(2)}) collective-permute-start(bf16[2,4352,128]{2,1,0:T(8,128)(2,1)} %get-tuple-element.190), channel_id=1, source_target_pairs={{0,1},{1,0},{2,3},{3,2},{4,5},{5,4},{6,7},{7,6},{8,9},{9,8},{10,11... | collective-permute-start | bytes 6684680 | tf_op jit(solution)/shard_map/ppermute | solution.py:72
  158.8 2.7 collective-permute-done.8
  161.5 3.4 %fusion = bf16[4352,128]{1,0:T(8,128)(2,1)} fusion(bf16[2,4352,128]{2,1,0:T(8,128)(2,1)S(1)} %collective-permute-done.8, bf16[2,4352,128]{2,1,0:T(8,128)(2,1)} %get-tuple-element.185), kind=kLoop, calls=%fused_computation.1 | loop fusion | flops 2228224 | bytes 3342336 | tf_op jit(solution)/shard_map/convert_element_type | solution.py:85
  164.9 1.8 collective-permute-start.10
  167.7 18.2 %shard_map.382 = (bf16[2048,512]{1,0:T(8,128)(2,1)}, bf16[2048,512]{1,0:T(8,128)(2,1)}, bf16[2048,1024]{1,0:T(8,128)(2,1)}) custom-call(f32[2]{0:T(128)} %decay.5, s32[2,1024]{1,0:T(2,128)} %seg_s.5, s32[2]{0:T(128)} %select_reduce_fusion.in_last, bf16[2048,512]{1,0:T(8,128)(2,1)} %get-tuple-element.155.refs_2_.refs_0_, ...), custom_call_target="tpu_custom_call" | custom-call | flops 9663676416 | bytes 33554432 | tf_op jit(solution)/shard_map/pallas_call | solution.py:770
  185.9 6.1 %collective-permute-done.10 = bf16[4352,128]{1,0:T(8,128)(2,1)S(1)} collective-permute-done((bf16[4352,128]{1,0:T(8,128)(2,1)}, bf16[4352,128]{1,0:T(8,128)(2,1)S(1)}, u32[]{:S(2)}, u32[]{:S(2)}) %collective-permute-start.10) | collective-permute-done | bytes 1114144 | tf_op jit(solution)/shard_map/ppermute | solution.py:72
  192.1 2.6 fusion.1
  196.4 8.7 %shard_map.383 = (bf16[2,1920,128]{2,1,0:T(8,128)(2,1)S(1)}, bf16[2,1920,128]{2,1,0:T(8,128)(2,1)S(1)}) custom-call(s32[3]{0:T(128)S(1)} %pad_add_fusion.me_ref.place, bf16[2048,512]{1,0:T(8,128)(2,1)S(1)} %copy-done.8, bf16[2048,512]{1,0:T(8,128)(2,1)S(1)} %copy-done.9, bf16[2048,1024]{1,0:T(8,128)(2,1)} %get-tuple-element.199.refs_2_.dv, ...), custom_call_target="tpu_custom_call" | custom-call | flops 3959422976 | bytes 10485760 | tf_op jit(solution)/shard_map/pallas_call | solution.py:684
  206.1 3.1 %collective-permute-done.11 = bf16[2176,128]{1,0:T(8,128)(2,1)} collective-permute-done((bf16[2176,128]{1,0:T(8,128)(2,1)}, bf16[2176,128]{1,0:T(8,128)(2,1)}, u32[]{:S(2)}, u32[]{:S(2)}) %collective-permute-start.11) | collective-permute-done | bytes 557088 | tf_op jit(solution)/shard_map/ppermute | solution.py:72
  218.2 6.1 %shard_map.384.rest_0_ = bf16[2048,512]{1,0:T(8,128)(2,1)} custom-call(bf16[2048,512]{1,0:T(8,128)(2,1)S(1)} %copy-done.8, bf16[2048,512]{1,0:T(8,128)(2,1)S(1)} %copy-done.10, bf16[2048,1024]{1,0:T(8,128)(2,1)S(1)} %copy-done.6, bf16[2048,1024]{1,0:T(8,128)(2,1)S(1)} %copy-done, bf16[2048,512]{1,0:T(8,128)(2,1)S(1)} %bitcast.74, ...), custom_call_target="tpu_custom_call" | custom-call | flops 3221225472 | bytes 10485760 | tf_op jit(solution)/shard_map/pallas_call | solution.py:812
  225.4 2.5 collective-permute-start.15
  227.9 6.3 %shard_map.385 = bf16[2048,512]{1,0:T(8,128)(2,1)} custom-call(bf16[2048,512]{1,0:T(8,128)(2,1)S(1)} %copy-done.8, bf16[2048,512]{1,0:T(8,128)(2,1)S(1)} %copy-done.10, bf16[2048,1024]{1,0:T(8,128)(2,1)S(1)} %copy-done.6, bf16[2048,1024]{1,0:T(8,128)(2,1)S(1)} %copy-done, bf16[2048,512]{1,0:T(8,128)(2,1)S(1)} %bitcast.75, ...), custom_call_target="tpu_custom_call", output_to_operand_aliasing={{}: (9, {})} | custom-call | flops 3221225472 | bytes 10485760 | tf_op jit(solution)/shard_map/pallas_call | solution.py:812
  236.0 2.7 collective-permute-done.15
  238.9 1.8 collective-permute-done.18
  241.4 7.0 %collective-permute-done.16 = bf16[1088,128]{1,0:T(8,128)(2,1)S(1)} collective-permute-done((bf16[1088,128]{1,0:T(8,128)(2,1)S(1)}, bf16[1088,128]{1,0:T(8,128)(2,1)S(1)}, u32[]{:S(2)}, u32[]{:S(2)}) %collective-permute-start.16) | collective-permute-done | bytes 278560 | tf_op jit(solution)/shard_map/ppermute | solution.py:72
  252.3 5.9 %collective-permute-done.20 = bf16[480,128]{1,0:T(8,128)(2,1)S(1)} collective-permute-done((bf16[480,128]{1,0:T(8,128)(2,1)S(1)}, bf16[480,128]{1,0:T(8,128)(2,1)S(1)}, u32[]{:S(2)}, u32[]{:S(2)}) %collective-permute-start.20) | collective-permute-done | bytes 122912 | tf_op jit(solution)/shard_map/ppermute | solution.py:72
  258.3 5.1 %collective-permute-done.21 = bf16[480,128]{1,0:T(8,128)(2,1)S(1)} collective-permute-done((bf16[480,128]{1,0:T(8,128)(2,1)S(1)}, bf16[480,128]{1,0:T(8,128)(2,1)S(1)}, u32[]{:S(2)}, u32[]{:S(2)}) %collective-permute-start.21) | collective-permute-done | bytes 122912 | tf_op jit(solution)/shard_map/ppermute | solution.py:72
  265.2 5.2 %collective-permute-done.22.refs_3_ = bf16[960,128]{1,0:T(8,128)(2,1)S(1)} collective-permute-done((bf16[960,128]{1,0:T(8,128)(2,1)S(1)}, bf16[960,128]{1,0:T(8,128)(2,1)S(1)}, u32[]{:S(2)}, u32[]{:S(2)}) %collective-permute-start.22) | collective-permute-done | bytes 245792 | tf_op jit(solution)/shard_map/ppermute | solution.py:72
  275.7 8.4 %shard_map.387 = (f32[2,128,512]{2,1,0:T(8,128)}, f32[2,864,128]{2,1,0:T(8,128)}, f32[864,128]{1,0:T(8,128)}, f32[2,864,128]{2,1,0:T(8,128)}, f32[864,128]{1,0:T...) custom-call(f32[8,128]{1,0:T(8,128)S(1)} %get-tuple-element.226.refs, ...), custom_call_target="tpu_custom_call" | custom-call | tf_op jit(solution)/shard_map/pallas_call | solution.py:938
  (175 shorter events, 53.9 us)
Async XLA Ops:
  7.2 56.3 %all-gather.2.cloned.1.call-start = ((), (), s32[]{:S(2)}) async-start(), calls=%async_computation | async-start | bytes 5939200 | tf_op jit(solution)/shard_map/all_gather | solution.py:1012
  9.4 14.1 %collective-permute-start = (bf16[1904,128]{1,0:T(8,128)(2,1)S(1)}, bf16[1904,128]{1,0:T(8,128)(2,1)S(1)}, u32[]{:S(2)}, u32[]{:S(2)}) collective-permute-start(bf16[1904,128]{1,0:T(8,128)(2,1)S(1)} %fusion.7.refs_0_), channel_id=1, source_target_pairs={{0,2},{1,3},{2,0},{3,1},{4,6},{5,7},{6,4},{7,5},{8,10},{9,11},{10,... | collective-permute-start | bytes 1462280 | tf_op jit(solution)/shard_map/ppermute | solution.py:72
  23.6 2.0 collective-permute-start.1
  23.7 2.5 collective-permute-start.2
  38.8 4.5 %collective-permute-start.3 = (bf16[2,2,256,512]{3,2,1,0:T(8,128)(2,1)}, bf16[2,2,256,512]{3,2,1,0:T(8,128)(2,1)S(1)}, u32[]{:S(2)}, u32[]{:S(2)}) collective-permute-start(bf16[2,2,256,512]{3,2,1,0:T(8,128)(2,1)} %get-tuple-element.144.local), channel_id=1, source_target_pairs={{0,1},{2,3},{4,5},{6,7},{8,9},{10,11},{12,13},{14,15},{16,17},{18,... | collective-permute-start | bytes 3145736 | tf_op jit(solution)/shard_map/ppermute | solution.py:143
  48.1 11.4 %collective-permute-start.4 = (bf16[2,2,256,512]{3,2,1,0:T(8,128)(2,1)}, bf16[2,2,256,512]{3,2,1,0:T(8,128)(2,1)S(1)}, u32[]{:S(2)}, u32[]{:S(2)}) collective-permute-start(bf16[2,2,256,512]{3,2,1,0:T(8,128)(2,1)} %shard_map.375), channel_id=1, source_target_pairs={{1,2},{5,6},{9,10},{13,14},{17,18},{21,22},{25,26},{29,30}} | collective-permute-start | bytes 3145736 | tf_op jit(solution)/shard_map/ppermute | solution.py:148
  59.4 10.2 %collective-permute-start.5 = (bf16[2,2,256,512]{3,2,1,0:T(8,128)(2,1)S(1)}, bf16[2,2,256,512]{3,2,1,0:T(8,128)(2,1)S(1)}, u32[]{:S(2)}, u32[]{:S(2)}) collective-permute-start(bf16[2,2,256,512]{3,2,1,0:T(8,128)(2,1)S(1)} %collective-permute-done.4.refs_9_), channel_id=1, source_target_pairs={{2,3},{6,7},{10,11},{14,15},{18,19},{22,23},{26,27},{30,31}} | collective-permute-start | bytes 3145736 | tf_op jit(solution)/shard_map/ppermute | solution.py:152
  70.6 43.3 %copy-start.37 = (bf16[2,1024,512]{2,1,0:T(8,128)(2,1)S(1)}, bf16[2,1024,512]{2,1,0:T(8,128)(2,1)}, u32[]{:S(2)}) copy-start(bf16[2,1024,512]{2,1,0:T(8,128)(2,1)} %param.23) | copy-start | bytes 6291460
  112.4 14.9 %collective-permute-start.6 = (bf16[2,2,256,512]{3,2,1,0:T(8,128)(2,1)}, bf16[2,2,256,512]{3,2,1,0:T(8,128)(2,1)S(1)}, u32[]{:S(2)}, u32[]{:S(2)}) collective-permute-start(bf16[2,2,256,512]{3,2,1,0:T(8,128)(2,1)} %get-tuple-element.167.local), channel_id=1, source_target_pairs={{3,2},{1,0},{7,6},{5,4},{11,10},{9,8},{15,14},{13,12},{19,18},{17,... | collective-permute-start | bytes 3145736 | tf_op jit(solution)/shard_map/ppermute | solution.py:143
  132.0 14.7 %collective-permute-start.7 = (bf16[2,2,256,512]{3,2,1,0:T(8,128)(2,1)}, bf16[2,2,256,512]{3,2,1,0:T(8,128)(2,1)S(1)}, u32[]{:S(2)}, u32[]{:S(2)}) collective-permute-start(bf16[2,2,256,512]{3,2,1,0:T(8,128)(2,1)} %shard_map.380), channel_id=1, source_target_pairs={{2,1},{6,5},{10,9},{14,13},{18,17},{22,21},{26,25},{30,29}} | collective-permute-start | bytes 3145736 | tf_op jit(solution)/shard_map/ppermute | solution.py:148
  146.7 14.8 %collective-permute-start.8 = (bf16[2,4352,128]{2,1,0:T(8,128)(2,1)}, bf16[2,4352,128]{2,1,0:T(8,128)(2,1)S(1)}, u32[]{:S(2)}, u32[]{:S(2)}) collective-permute-start(bf16[2,4352,128]{2,1,0:T(8,128)(2,1)} %get-tuple-element.190), channel_id=1, source_target_pairs={{0,1},{1,0},{2,3},{3,2},{4,5},{5,4},{6,7},{7,6},{8,9},{9,8},{10,11... | collective-permute-start | bytes 6684680 | tf_op jit(solution)/shard_map/ppermute | solution.py:72
  157.3 9.4 %collective-permute-start.9 = (bf16[2,2,256,512]{3,2,1,0:T(8,128)(2,1)S(1)}, bf16[2,2,256,512]{3,2,1,0:T(8,128)(2,1)S(1)}, u32[]{:S(2)}, u32[]{:S(2)}) collective-permute-start(bf16[2,2,256,512]{3,2,1,0:T(8,128)(2,1)S(1)} %collective-permute-done.7.refs_11_), channel_id=1, source_target_pairs={{1,0},{5,4},{9,8},{13,12},{17,16},{21,20},{25,24},{29,28}} | collective-permute-start | bytes 3145736 | tf_op jit(solution)/shard_map/ppermute | solution.py:152
  164.9 27.1 %collective-permute-start.10 = (bf16[4352,128]{1,0:T(8,128)(2,1)}, bf16[4352,128]{1,0:T(8,128)(2,1)S(1)}, u32[]{:S(2)}, u32[]{:S(2)}) collective-permute-start(bf16[4352,128]{1,0:T(8,128)(2,1)} %fusion), channel_id=1, source_target_pairs={{0,2},{1,3},{2,0},{3,1},{4,6},{5,7},{6,4},{7,5},{8,10},{9,11},{10,... | collective-permute-start | bytes 3342344 | tf_op jit(solution)/shard_map/ppermute | solution.py:72
  194.7 14.5 %collective-permute-start.11 = (bf16[2176,128]{1,0:T(8,128)(2,1)}, bf16[2176,128]{1,0:T(8,128)(2,1)}, u32[]{:S(2)}, u32[]{:S(2)}) collective-permute-start(bf16[2176,128]{1,0:T(8,128)(2,1)} %get-tuple-element.250), channel_id=1, source_target_pairs={{0,4},{4,0},{8,12},{12,8},{16,20},{20,16},{24,28},{28,24},{1,5},{5... | collective-permute-start | bytes 1671176 | tf_op jit(solution)/shard_map/ppermute | solution.py:72
  206.1 6.0 %collective-permute-start.12 = (bf16[2,1920,128]{2,1,0:T(8,128)(2,1)S(1)}, bf16[2,1920,128]{2,1,0:T(8,128)(2,1)S(1)}, u32[]{:S(2)}, u32[]{:S(2)}) collective-permute-start(bf16[2,1920,128]{2,1,0:T(8,128)(2,1)S(1)} %get-tuple-element.213), channel_id=1, source_target_pairs={{0,1},{1,0},{2,3},{3,2},{4,5},{5,4},{6,7},{7,6},{8,9},{9,8},{10,11... | collective-permute-start | bytes 2949128 | tf_op jit(solution)/shard_map/ppermute | solution.py:72
  210.3 14.0 %collective-permute-start.13 = (bf16[1088,128]{1,0:T(8,128)(2,1)S(1)}, bf16[1088,128]{1,0:T(8,128)(2,1)S(1)}, u32[]{:S(2)}, u32[]{:S(2)}) collective-permute-start(bf16[1088,128]{1,0:T(8,128)(2,1)S(1)} %add_convert_fusion.5), channel_id=1, source_target_pairs={{0,8},{4,12},{8,0},{12,4},{16,24},{20,28},{24,16},{28,20},{1,9},{5... | collective-permute-start | bytes 835592 | tf_op jit(solution)/shard_map/ppermute | solution.py:72
  213.3 20.9 %collective-permute-start.14 = (bf16[1920,128]{1,0:T(8,128)(2,1)S(1)}, bf16[1920,128]{1,0:T(8,128)(2,1)S(1)}, u32[]{:S(2)}, u32[]{:S(2)}) collective-permute-start(bf16[1920,128]{1,0:T(8,128)(2,1)S(1)} %fusion.4), channel_id=1, source_target_pairs={{0,2},{1,3},{2,0},{3,1},{4,6},{5,7},{6,4},{7,5},{8,10},{9,11},{10,... | collective-permute-start | bytes 1474568 | tf_op jit(solution)/shard_map/ppermute | solution.py:72
  225.4 13.3 %collective-permute-start.15 = (bf16[1088,128]{1,0:T(8,128)(2,1)S(1)}, bf16[1088,128]{1,0:T(8,128)(2,1)S(1)}, u32[]{:S(2)}, u32[]{:S(2)}) collective-permute-start(bf16[1088,128]{1,0:T(8,128)(2,1)S(1)} %add_convert_fusion.3), channel_id=1, source_target_pairs={{0,16},{4,20},{8,24},{12,28},{16,0},{20,4},{24,8},{28,12},{1,17},{... | collective-permute-start | bytes 835592 | tf_op jit(solution)/shard_map/ppermute | solution.py:72
  234.2 41.3 %copy-start.27 = (f32[2,128,512]{2,1,0:T(8,128)S(1)}, f32[2,128,512]{2,1,0:T(8,128)}, u32[]{:S(2)}) copy-start(f32[2,128,512]{2,1,0:T(8,128)} %refs_19_.1) | copy-start | bytes 1572868
  234.2 41.3 %copy-start.28 = (f32[864,128]{1,0:T(8,128)S(1)}, f32[864,128]{1,0:T(8,128)}, u32[]{:S(2)}) copy-start(f32[864,128]{1,0:T(8,128)} %refs_15_.1) | copy-start | bytes 1327108
  234.2 41.3 %copy-start.29 = (f32[864,128]{1,0:T(8,128)S(1)}, f32[864,128]{1,0:T(8,128)}, u32[]{:S(2)}) copy-start(f32[864,128]{1,0:T(8,128)} %refs_17_.1) | copy-start | bytes 1327108
  234.3 41.3 %copy-start.30 = (f32[864,128]{1,0:T(8,128)S(1)}, f32[864,128]{1,0:T(8,128)}, u32[]{:S(2)}) copy-start(f32[864,128]{1,0:T(8,128)} %refs_21_.1) | copy-start | bytes 1327108
  234.5 6.3 %collective-permute-start.18 = (bf16[960,128]{1,0:T(8,128)(2,1)S(1)}, bf16[960,128]{1,0:T(8,128)(2,1)S(1)}, u32[]{:S(2)}, u32[]{:S(2)}) collective-permute-start(bf16[960,128]{1,0:T(8,128)(2,1)S(1)} %get-tuple-element.252), channel_id=1, source_target_pairs={{0,4},{4,0},{8,12},{12,8},{16,20},{20,16},{24,28},{28,24},{1,5},{5... | collective-permute-start | bytes 737288 | tf_op jit(solution)/shard_map/ppermute | solution.py:72
  238.8 9.6 %collective-permute-start.16 = (bf16[1088,128]{1,0:T(8,128)(2,1)S(1)}, bf16[1088,128]{1,0:T(8,128)(2,1)S(1)}, u32[]{:S(2)}, u32[]{:S(2)}) collective-permute-start(bf16[1088,128]{1,0:T(8,128)(2,1)S(1)} %add_convert_fusion.2), channel_id=1, source_target_pairs={{0,8},{4,12},{8,0},{12,4},{16,24},{20,28},{24,16},{28,20},{1,9},{5... | collective-permute-start | bytes 835592 | tf_op jit(solution)/shard_map/ppermute | solution.py:72
  240.8 9.3 %collective-permute-start.19 = (bf16[480,128]{1,0:T(8,128)(2,1)S(1)}, bf16[480,128]{1,0:T(8,128)(2,1)S(1)}, u32[]{:S(2)}, u32[]{:S(2)}) collective-permute-start(bf16[480,128]{1,0:T(8,128)(2,1)S(1)} %add_convert_fusion.8), channel_id=1, source_target_pairs={{0,8},{4,12},{8,0},{12,4},{16,24},{20,28},{24,16},{28,20},{1,9},{5... | collective-permute-start | bytes 368648 | tf_op jit(solution)/shard_map/ppermute | solution.py:72
  250.2 8.0 %collective-permute-start.20 = (bf16[480,128]{1,0:T(8,128)(2,1)S(1)}, bf16[480,128]{1,0:T(8,128)(2,1)S(1)}, u32[]{:S(2)}, u32[]{:S(2)}) collective-permute-start(bf16[480,128]{1,0:T(8,128)(2,1)S(1)} %add_convert_fusion.7), channel_id=1, source_target_pairs={{0,16},{4,20},{8,24},{12,28},{16,0},{20,4},{24,8},{28,12},{1,17},{... | collective-permute-start | bytes 368648 | tf_op jit(solution)/shard_map/ppermute | solution.py:72
  250.7 14.5 %collective-permute-start.17 = (bf16[2176,128]{1,0:T(8,128)(2,1)S(1)}, bf16[2176,128]{1,0:T(8,128)(2,1)S(1)}, u32[]{:S(2)}, u32[]{:S(2)}) collective-permute-start(bf16[2176,128]{1,0:T(8,128)(2,1)S(1)} %pad_maximum_fusion.refs_0_), channel_id=1, source_target_pairs={{0,4},{4,0},{8,12},{12,8},{16,20},{20,16},{24,28},{28,24},{1,5},{5... | collective-permute-start | bytes 1671176 | tf_op jit(solution)/shard_map/ppermute | solution.py:72
  258.2 5.2 %collective-permute-start.21 = (bf16[480,128]{1,0:T(8,128)(2,1)S(1)}, bf16[480,128]{1,0:T(8,128)(2,1)S(1)}, u32[]{:S(2)}, u32[]{:S(2)}) collective-permute-start(bf16[480,128]{1,0:T(8,128)(2,1)S(1)} %add_convert_fusion.6), channel_id=1, source_target_pairs={{0,8},{4,12},{8,0},{12,4},{16,24},{20,28},{24,16},{28,20},{1,9},{5... | collective-permute-start | bytes 368648 | tf_op jit(solution)/shard_map/ppermute | solution.py:72
  263.4 7.0 %collective-permute-start.22 = (bf16[960,128]{1,0:T(8,128)(2,1)S(1)}, bf16[960,128]{1,0:T(8,128)(2,1)S(1)}, u32[]{:S(2)}, u32[]{:S(2)}) collective-permute-start(bf16[960,128]{1,0:T(8,128)(2,1)S(1)} %pad_maximum_fusion.1.refs_2_), channel_id=1, source_target_pairs={{0,4},{4,0},{8,12},{12,8},{16,20},{20,16},{24,28},{28,24},{1,5},{5... | collective-permute-start | bytes 737288 | tf_op jit(solution)/shard_map/ppermute | solution.py:72
  271.9 3.0 %collective-permute-start.25 = (f32[8,128]{1,0:T(8,128)S(1)}, f32[8,128]{1,0:T(8,128)S(1)}, u32[]{:S(2)}, u32[]{:S(2)}) collective-permute-start(f32[8,128]{1,0:T(8,128)S(1)} %get-tuple-element.226.refs_0_), channel_id=1, source_target_pairs={{0,3},{1,2},{2,1},{3,0},{4,7},{5,6},{6,5},{7,4},{8,11},{9,10},{10,... | collective-permute-start | bytes 12296 | tf_op jit(solution)/shard_map/ppermute | solution.py:1091
  271.9 3.7 %collective-permute-start.24 = (f32[8,128]{1,0:T(8,128)S(1)}, f32[8,128]{1,0:T(8,128)S(1)}, u32[]{:S(2)}, u32[]{:S(2)}) collective-permute-start(f32[8,128]{1,0:T(8,128)S(1)} %get-tuple-element.226.refs_0_), channel_id=1, source_target_pairs={{0,2},{1,3},{2,0},{3,1},{4,6},{5,7},{6,4},{7,5},{8,10},{9,11},{10,... | collective-permute-start | bytes 12296 | tf_op jit(solution)/shard_map/ppermute | solution.py:1091
  272.4 3.1 %collective-permute-start.23 = (f32[8,128]{1,0:T(8,128)S(1)}, f32[8,128]{1,0:T(8,128)S(1)}, u32[]{:S(2)}, u32[]{:S(2)}) collective-permute-start(f32[8,128]{1,0:T(8,128)S(1)} %get-tuple-element.226.refs_0_), channel_id=1, source_target_pairs={{0,1},{1,0},{2,3},{3,2},{4,5},{5,4},{6,7},{7,6},{8,9},{9,8},{10,11... | collective-permute-start | bytes 12296 | tf_op jit(solution)/shard_map/ppermute | solution.py:1091
  (45 other events, 456.6 us)
Sparse Core Ops, SparseCore 0:
  23.7 39.7 all-gather.1
